TPU v7x, 128 devices: a whole 4x4x4 slice. The times are simulated.
128 devices in a mesh: section: 4 (over x), ctx: 16 (over y, z), tp: 2 (over core).
Axes of the slice: x: 4, y: 4, z: 4, core: 2. Of those that a mesh axis runs over, the one named last changes fastest.
Arguments:
- prefill_hidden_states: bfloat16 [32768, 8192], P(('section', 'ctx')), may hold values from -6 to 6
- decode_hidden_states: bfloat16 [2, 16, 8192], P(None, 'section', 'ctx'), may hold values from -6 to 6
- query_matrix: bfloat16 [8192, 8192], P('ctx', 'tp'), may hold values from -0.0625 to 0.0625
- key_matrix: bfloat16 [8192, 1024], P('ctx', 'tp'), may hold values from -0.0625 to 0.0625
- value_matrix: bfloat16 [8192, 1024], P('ctx', 'tp'), may hold values from -0.0625 to 0.0625
- adapter_down_maps: bfloat16 [8192, 256], P('ctx', 'tp'), may hold values from -0.0625 to 0.0625
- key_adapter_up_maps: bfloat16 [128, 1024], P(None, 'tp'), may hold values from -1.5 to 1.5
- value_adapter_up_maps: bfloat16 [128, 1024], P(None, 'tp'), may hold values from -1.5 to 1.5
- request_key_cache: bfloat16 [16, 16384, 1024], P('section', 'ctx', 'tp'), may hold values from -1000 to 1000
- request_value_cache: bfloat16 [16, 16384, 1024], P('section', 'ctx', 'tp'), may hold values from -6 to 6
- request_adapter_index: int32 [16], replicated, may hold values from 0 to 7
- prefill_request_target: int32 [4], replicated, may hold values from 0 to 15, as said below
- request_context_length: int32 [16], P('section'), may hold values from 1024 to 16384, as said below
- page_owner_index: int32 [1024, 1], P(('section', 'ctx')), may hold values from 0 to 15; in each aligned block of 16 rows (0 to 15, 16 to 31, ...) at most 2 rows name the same one
Outputs:
- page_keys: bfloat16 [2048, 32, 1024], P(('section', 'ctx'), None, 'tp')
- page_values: bfloat16 [2048, 32, 1024], P(('section', 'ctx'), None, 'tp')
- attended: bfloat16 [2, 16, 8192], P(None, 'section', 'tp')
Inputs may be any that keep to these rules, and one draw needn't show every extreme that they name: `prefill_request_target`: entry j names one of the 4 requests of decode group (j + 1) mod 4, i.e. a value of ((j + 1) mod 4) * 4 to that plus 4 - 1; one entry names request 0, another the last request. `request_context_length`: one request of every draw has all 16384 positions live, another exactly 1024. `page_owner_index`: among the 16 pages of one device, no owner is named more than 2 times.
All inputs are finite; a program needn't handle non-finite values.
Results may differ from a plain program's by a relative error of at most 0.0095.
Values may be sent and summed in bfloat16 or wider, within the bound.
A program may use at most 192 MiB of HBM per device.

v0:
```python
import jax
import jax.numpy as jnp
from jax import lax
from jax.sharding import PartitionSpec as P

H = 64
KVH = 8
HD = 128
ADAPTER_RANK = 16
BLK = 32
STEPS = 2


ADAPTER_SCALE = 0.5
NEG_FLOOR = -1e30


def shifted(value, axis, by):
    peers = lax.axis_size(axis)
    return lax.ppermute(value, axis, [(i, (i + by) % peers) for i in range(peers)])


def add_adapter_delta(base_projection, down_columns_half, token_adapter_indices, adapter_up_maps):
    column_adapter = jnp.arange(down_columns_half.shape[1], dtype=jnp.int32) // ADAPTER_RANK
    select = column_adapter[None, :] == token_adapter_indices[:, None]
    selected_maps = jnp.where(select, down_columns_half, jnp.zeros_like(down_columns_half))
    adapter_delta = jnp.dot(selected_maps, adapter_up_maps, preferred_element_type=jnp.float32)
    return (base_projection + ADAPTER_SCALE * adapter_delta).astype(jnp.bfloat16)


def pick_entry(table, wanted):
    places = jnp.arange(table.shape[0], dtype=jnp.int32)
    return jnp.sum(jnp.where(places == wanted, table, 0))


def on_device(
    prefill_hidden_states,
    decode_hidden_states,
    query_matrix,
    key_matrix,
    value_matrix,
    adapter_down_maps,
    key_adapter_up_maps,
    value_adapter_up_maps,
    request_key_cache,
    request_value_cache,
    request_adapter_index,
    prefill_request_target,
    request_context_length,
    page_owner_index,
):
    n_ctx = lax.axis_size("ctx")
    n_section = lax.axis_size("section")
    section_at = lax.axis_index("section")
    ctx_at = lax.axis_index("ctx")
    row_count = prefill_hidden_states.shape[0]
    reduced_rank_product = adapter_down_maps.shape[1]
    head_cols = key_matrix.shape[1]
    span_request = pick_entry(prefill_request_target, section_at)
    span_adapter = pick_entry(request_adapter_index, span_request)
    pieces = (
        lax.all_gather(key_matrix, "ctx", axis=0, tiled=True),
        lax.all_gather(value_matrix, "ctx", axis=0, tiled=True),
        lax.all_gather(adapter_down_maps, "ctx", axis=0, tiled=True),
    )
    plain_projected_keys, plain_projected_values, down_columns_half = tuple(
        (
            jnp.dot(prefill_hidden_states, piece, preferred_element_type=jnp.float32)
            for piece in pieces
        )
    )
    prefill_down_product = lax.all_gather(
        down_columns_half.astype(jnp.bfloat16), "tp", axis=1, tiled=True
    )
    token_adapter_indices = jnp.full((row_count,), span_adapter, jnp.int32)
    prefill_key_rows = add_adapter_delta(
        plain_projected_keys,
        prefill_down_product[:, :reduced_rank_product],
        token_adapter_indices,
        key_adapter_up_maps,
    )
    prefill_value_rows = add_adapter_delta(
        plain_projected_values,
        prefill_down_product[:, reduced_rank_product:],
        token_adapter_indices,
        value_adapter_up_maps,
    )
    block_count = row_count // BLK
    send_most = max(2, 2 * block_count // n_ctx)
    slot_total = n_ctx * send_most
    owners = page_owner_index[:, 0]
    order = jnp.arange(block_count, dtype=jnp.int32)
    same_owner = owners[None, :] == owners[:, None]
    earlier = order[None, :] < order[:, None]
    rank = jnp.sum(jnp.logical_and(same_owner, earlier), axis=1)
    slot_of = owners * send_most + rank
    placing = (slot_of[None, :] == jnp.arange(slot_total, dtype=jnp.int32)[:, None]).astype(
        jnp.bfloat16
    )

    def place(rows):
        blocks = rows.reshape(block_count, BLK * head_cols)
        placed = jnp.dot(placing, blocks, preferred_element_type=jnp.float32).astype(jnp.bfloat16)
        return placed.reshape(n_ctx, send_most, BLK, head_cols)

    send_keys = place(prefill_key_rows)
    send_values = place(prefill_value_rows)
    send_flags = (
        jnp.sum(placing.astype(jnp.float32), axis=1).astype(jnp.bfloat16).reshape(n_ctx, send_most)
    )
    moved_keys, moved_values, moved_flags = shifted(
        (send_keys, send_values, send_flags), "section", 1
    )
    page_keys, page_values, page_flags = (
        lax.all_to_all(moved_keys, "ctx", split_axis=0, concat_axis=0, tiled=True),
        lax.all_to_all(moved_values, "ctx", split_axis=0, concat_axis=0, tiled=True),
        lax.all_to_all(moved_flags, "ctx", split_axis=0, concat_axis=0, tiled=True),
    )
    page_keys = page_keys.reshape(slot_total, BLK, head_cols)
    page_values = page_values.reshape(slot_total, BLK, head_cols)
    group_size = request_context_length.shape[0]
    local_ids = section_at * group_size + jnp.arange(group_size, dtype=jnp.int32)
    batch_ids = jnp.arange(request_adapter_index.shape[0], dtype=jnp.int32)
    resident_adapter_table = jnp.sum(
        jnp.where(local_ids[:, None] == batch_ids[None, :], request_adapter_index[None, :], 0),
        axis=1,
    )
    page_request = pick_entry(prefill_request_target, (section_at + n_section - 1) % n_section)
    page_live = jnp.repeat(page_flags.reshape(slot_total) > 0.5, BLK)
    ctx_len = request_key_cache.shape[1]
    positions = ctx_at * ctx_len + jnp.arange(ctx_len, dtype=jnp.int32)
    cache_live = positions[None, :] < request_context_length[:, None]
    page_for = jnp.logical_and((local_ids == page_request)[:, None], page_live[None, :])
    live_wide = jnp.concatenate([cache_live, page_for], axis=1)[:, None, None, :]
    kv_heads = head_cols // HD
    group_heads = H // KVH
    cache_k = request_key_cache.reshape(group_size, ctx_len, kv_heads, HD)
    cache_v = request_value_cache.reshape(group_size, ctx_len, kv_heads, HD)
    page_k = page_keys.reshape(slot_total * BLK, kv_heads, HD)
    page_v = page_values.reshape(slot_total * BLK, kv_heads, HD)
    inv_root = HD ** (-0.5)
    decode_key_rows = []
    decode_value_rows = []
    attended = []
    for step in range(STEPS):
        step_hidden_states = decode_hidden_states[step]
        running_sums = lax.psum(
            (
                jnp.dot(step_hidden_states, query_matrix, preferred_element_type=jnp.float32),
                jnp.dot(step_hidden_states, key_matrix, preferred_element_type=jnp.float32),
                jnp.dot(step_hidden_states, value_matrix, preferred_element_type=jnp.float32),
                jnp.dot(step_hidden_states, adapter_down_maps, preferred_element_type=jnp.float32),
            ),
            "ctx",
        )
        decode_down_product = lax.all_gather(
            running_sums[3].astype(jnp.bfloat16), "tp", axis=1, tiled=True
        )
        queries = (
            running_sums[0].astype(jnp.bfloat16).reshape(group_size, kv_heads, group_heads, HD)
        )
        decode_key_rows.append(
            add_adapter_delta(
                running_sums[1],
                decode_down_product[:, :reduced_rank_product],
                resident_adapter_table,
                key_adapter_up_maps,
            )
        )
        decode_value_rows.append(
            add_adapter_delta(
                running_sums[2],
                decode_down_product[:, reduced_rank_product:],
                resident_adapter_table,
                value_adapter_up_maps,
            )
        )
        cache_scores = jnp.einsum(
            "bkgd,bpkd->bkgp", queries, cache_k, preferred_element_type=jnp.float32
        )
        page_scores = jnp.einsum(
            "bkgd,pkd->bkgp", queries, page_k, preferred_element_type=jnp.float32
        )
        scores = jnp.concatenate([cache_scores, page_scores], axis=3) * inv_root
        block_max = jnp.max(jnp.where(live_wide, scores, NEG_FLOOR), axis=3)
        weights = jnp.where(live_wide, jnp.exp(scores - block_max[..., None]), 0.0).astype(
            jnp.bfloat16
        )
        block_total = jnp.sum(weights.astype(jnp.float32), axis=3)
        block_out = jnp.einsum(
            "bkgp,bpkd->bkgd", weights[..., :ctx_len], cache_v, preferred_element_type=jnp.float32
        )
        block_out = block_out + jnp.einsum(
            "bkgp,pkd->bkgd", weights[..., ctx_len:], page_v, preferred_element_type=jnp.float32
        )
        merged_max = lax.pmax(block_max, "ctx")
        factor = jnp.exp(block_max - merged_max)
        merged_total, merged_out = lax.psum(
            (block_total * factor, block_out * factor[..., None]), "ctx"
        )
        stacked_k = jnp.stack(decode_key_rows, axis=1).reshape(group_size, step + 1, kv_heads, HD)
        stacked_v = jnp.stack(decode_value_rows, axis=1).reshape(group_size, step + 1, kv_heads, HD)
        token_scores = (
            jnp.einsum("bkgd,bukd->bkgu", queries, stacked_k, preferred_element_type=jnp.float32)
            * inv_root
        )
        top = jnp.maximum(merged_max, jnp.max(token_scores, axis=3))
        block_scale = jnp.exp(merged_max - top)
        token_weights = jnp.exp(token_scores - top[..., None])
        numer = merged_out * block_scale[..., None] + jnp.einsum(
            "bkgu,bukd->bkgd", token_weights, stacked_v.astype(jnp.float32)
        )
        denom = merged_total * block_scale + jnp.sum(token_weights, axis=3)
        attended.append(
            (numer / denom[..., None])
            .astype(jnp.bfloat16)
            .reshape(group_size, kv_heads * group_heads * HD)
        )
    return (page_keys, page_values, jnp.stack(attended, axis=0))


def solution(mesh):
    return jax.shard_map(
        on_device,
        mesh=mesh,
        in_specs=(
            P(("section", "ctx"), None),
            P(None, "section", "ctx"),
            P("ctx", "tp"),
            P("ctx", "tp"),
            P("ctx", "tp"),
            P("ctx", "tp"),
            P(None, "tp"),
            P(None, "tp"),
            P("section", "ctx", "tp"),
            P("section", "ctx", "tp"),
            P(),
            P(),
            P("section"),
            P(("section", "ctx"), None),
        ),
        out_specs=(
            P(("section", "ctx"), None, "tp"),
            P(("section", "ctx"), None, "tp"),
            P(None, "section", "tp"),
        ),
        check_vma=False,
    )
```

profile of v0, /device:TPU:0, one launch (start us, length us, event | category | flops | bytes accessed | tf_op | source)
XLA Modules:
  0.0 501.9 jit_solution(12365704744188621446)
XLA Ops:
  7.2 0.7 all-gather.6.cloned.1.call-update
  8.0 0.7 all-gather.4.cloned.1.call-update
  8.7 0.7 all-gather.8.cloned.1.call-update
  9.4 0.9 convert_reduce_fusion.2
  11.2 1.6 collective-permute-start.2
  12.8 3.0 fusion.78
  16.9 77.9 %all-reduce.8 = (bf16[4,4096]{1,0:T(4,128)(2,1)}, bf16[4,4096]{1,0:T(4,128)(2,1)S(1)}) all-reduce(f32[4,4096]{1,0:T(4,128)S(1)} %fusion.78, f32[4,4096]{1,0:T(4,128)S(1)} %fusion.86), channel_id=1, replica_groups=mesh['section'=4,'ctx'=16,'tp'=2] {'ctx'}, use_global_device_ids=true, to_apply=%region_15.16 | all-reduce | flops 32768 | bytes 196608 | tf_op jit(solution)/shard_map/psum | solution.py:147
  96.0 1.3 fusion.111
  97.3 0.8 select_reduce_fusion.2
  98.1 0.7 fusion.74
  98.8 0.7 fusion.82
  99.9 0.8 fusion.72
  100.7 0.8 fusion.80
  101.5 4.2 fusion.6
  106.9 4.1 all-to-all-start.2
  111.0 6.5 %convolution_convert_fusion.2 = bf16[512,128]{1,0:T(8,128)(2,1)S(1)} fusion(bf16[512,8192]{1,0:T(8,128)(2,1)} %param.14, bf16[8192,128]{1,0:T(8,128)(2,1)} %all-gather.6.cloned.1.call-done), kind=kOutput, calls=%fused_computation.22 | convolution fusion | flops 1073807360 | bytes 10616832 | tf_op jit(solution)/shard_map/dot_general | solution.py:68
  117.5 2.0 all_gather.20
  119.5 11.1 %all-gather.4.cloned.1.call-done = bf16[8192,512]{1,0:T(8,128)(2,1)} async-done(((bf16[512,512]{1,0:T(8,128)(2,1)}), bf16[8192,512]{1,0:T(8,128)(2,1)}) %all-gather.4.cloned.1.call-update) | async-done | bytes 8388624 | tf_op jit(solution)/shard_map/all_gather | solution.py:62
  130.7 9.4 %fusion.130 = f32[512,512]{1,0:T(8,128)S(1)} fusion(bf16[512,8192]{1,0:T(8,128)(2,1)} %param.14, bf16[8192,512]{1,0:T(8,128)(2,1)} %all-gather.4.cloned.1.call-done), kind=kOutput, calls=%fused_computation.190 | convolution fusion | flops 4294967296 | bytes 17825792 | tf_op jit(solution)/shard_map/dot_general | solution.py:68
  141.6 1.7 collective-permute-start
  143.3 60.0 %all-gather.8.cloned.1.call-done = bf16[8192,512]{1,0:T(8,128)(2,1)} async-done(((bf16[512,512]{1,0:T(8,128)(2,1)}), bf16[8192,512]{1,0:T(8,128)(2,1)}) %all-gather.8.cloned.1.call-update) | async-done | bytes 8388624 | tf_op jit(solution)/shard_map/all_gather | solution.py:63
  203.3 9.4 %fusion.131 = f32[512,512]{1,0:T(8,128)S(1)} fusion(bf16[512,8192]{1,0:T(8,128)(2,1)} %param.14, bf16[8192,512]{1,0:T(8,128)(2,1)} %all-gather.8.cloned.1.call-done), kind=kOutput, calls=%fused_computation.191 | convolution fusion | flops 4294967296 | bytes 17825792 | tf_op jit(solution)/shard_map/dot_general | solution.py:68
  213.3 1.2 convolution_convert_fusion
  214.9 1.5 collective-permute-start.1
  217.0 5.3 %all-to-all-start = ((bf16[16,2,32,512]{3,2,1,0:T(8,128)(2,1)}), bf16[16,2,32,512]{3,2,1,0:T(8,128)(2,1)S(1)}, u32[]{:S(2)}, u32[]{:S(2)}) async-start(bf16[16,2,32,512]{3,2,1,0:T(8,128)(2,1)} %collective-permute-done), calls=%async_computation | async-start | bytes 2097152 | tf_op jit(solution)/shard_map/all_to_all | solution.py:115
  222.8 4.2 fusion.4
  227.0 0.7 compare_reduce_fusion
  228.2 13.0 %collective-permute-done.1 = bf16[16,2,32,512]{3,2,1,0:T(8,128)(2,1)} collective-permute-done((bf16[16,2,32,512]{3,2,1,0:T(8,128)(2,1)S(1)}, bf16[16,2,32,512]{3,2,1,0:T(8,128)(2,1)}, u32[]{:S(2)}, u32[]{:S(2)}) %collective-permute-start.1) | collective-permute-done | bytes 1048608 | tf_op jit(solution)/shard_map/ppermute | solution.py:20
  241.2 5.3 %all-to-all-start.1 = ((bf16[16,2,32,512]{3,2,1,0:T(8,128)(2,1)}), bf16[16,2,32,512]{3,2,1,0:T(8,128)(2,1)S(1)}, u32[]{:S(2)}, u32[]{:S(2)}) async-start(bf16[16,2,32,512]{3,2,1,0:T(8,128)(2,1)} %collective-permute-done.1), calls=%async_computation.1 | async-start | bytes 2097152 | tf_op jit(solution)/shard_map/all_to_all | solution.py:116
  247.8 1.6 select_reduce_fusion.1
  250.0 74.9 %all-reduce.3 = (f32[4,4,8]{2,1,0:T(4,128)S(1)}, f32[4,4,8]{2,1,0:T(4,128)S(1)}) all-reduce(f32[4,4,8]{2,1,0:T(4,128)S(1)} %get-tuple-element.4, f32[4,4,8]{2,1,0:T(4,128)S(1)} %get-tuple-element.3), channel_id=1, replica_groups=mesh['section'=4,'ctx'=16,'tp'=2] {'ctx'}, use_global_device_ids=true, to_apply=%region_17.18 | all-reduce | flops 256 | bytes 2048 | tf_op jit(solution)/shard_map/pmax | solution.py:196
  325.6 70.4 %all-reduce = (f32[4,512]{1,0:T(4,128)}, bf16[4,128]{1,0:T(4,128)(2,1)S(1)}, f32[4,512]{1,0:T(4,128)}, bf16[4,128]{1,0:T(4,128)(2,1)S(1)}, f32[4,4,8]{2,1,0:T(4,...) all-reduce(f32[4,512]{1,0:T(4,128)S(1)} %fusion.76, ...), channel_id=1, replica_groups=mesh['section'=4,'ctx'=16,'tp'=2] {'ctx'}, use_global_device_ids=true, to_apply=%region_19.20 | all-reduce | flops 9472 | bytes 73728 | tf_op jit(solution)/shard_map/psum | solution.py:147
  395.9 1.8 all_gather.23
  397.7 0.9 fusion.29
  398.6 0.9 fusion.28
  399.5 1.8 all_gather.22
  401.3 0.9 fusion.27
  402.2 0.9 fusion.26
  403.5 3.0 fusion.2
  407.5 1.1 reshape_reshape.7
  408.6 2.1 fusion.20
  410.8 2.1 fusion.18
  412.9 77.7 %all-reduce.7.cloned.1.call-done = (f32[4,4,8,128]{3,2,1,0:T(8,128)}, f32[4,4,8,128]{3,2,1,0:T(8,128)}) async-done(((f32[4,4,8,128]{3,2,1,0:T(8,128)}, f32[4,4,8,128]{3,2,1,0:T(8,128)}), (f32[4,4,8,128]{3,2,1,0:T(8,128)}, f32[4,4,8,128]{3,2,1,0:T(8,128)})) %all-reduce.7.cloned.1.call-update) | async-done | bytes 131088 | tf_op jit(solution)/shard_map/psum | solution.py:198
  490.7 1.1 fusion.21
  491.8 1.0 divide_convert_fusion
  492.8 0.7 pad_maximum_fusion
  493.4 1.0 copy.161
  494.4 1.0 copy.162
  (109 shorter events, 12.7 us)
Async XLA Ops:
  7.2 205.6 %copy-start = (bf16[128,512]{1,0:T(8,128)(2,1)S(1)}, bf16[128,512]{1,0:T(8,128)(2,1)}, u32[]{:S(2)}) copy-start(bf16[128,512]{1,0:T(8,128)(2,1)} %param.21) | copy-start | bytes 393220
  7.2 8.7 %copy-start.11 = (bf16[2,4,512]{2,1,0:T(4,128)(2,1)S(1)}, bf16[2,4,512]{2,1,0:T(4,128)(2,1)}, u32[]{:S(2)}) copy-start(bf16[2,4,512]{2,1,0:T(4,128)(2,1)} %param.15) | copy-start | bytes 24580
  7.2 103.8 %all-gather.6.cloned.1.call-start = ((), (), s32[]{:S(2)}) async-start(), calls=%async_computation.4 | async-start | bytes 2228224 | tf_op jit(solution)/shard_map/all_gather | solution.py:64
  7.9 122.7 %all-gather.4.cloned.1.call-start = ((), (), s32[]{:S(2)}) async-start(), calls=%async_computation.3 | async-start | bytes 8912896 | tf_op jit(solution)/shard_map/all_gather | solution.py:62
  8.7 194.6 %all-gather.8.cloned.1.call-start = ((), (), s32[]{:S(2)}) async-start(), calls=%async_computation.5 | async-start | bytes 8912896 | tf_op jit(solution)/shard_map/all_gather | solution.py:63
  11.0 129.7 %copy-start.20 = (s32[16]{0:T(128)}, s32[16]{0:T(128)S(1)}, u32[]{:S(2)}) copy-start(s32[16]{0:T(128)S(1)} %multiply_add_fusion.2) | copy-start | bytes 196
  11.2 95.1 %collective-permute-start.2 = (bf16[16,2]{1,0:T(8,128)(2,1)S(1)}, bf16[16,2]{1,0:T(8,128)(2,1)S(1)}, u32[]{:S(2)}, u32[]{:S(2)}) collective-permute-start(bf16[16,2]{1,0:T(8,128)(2,1)S(1)} %reshape.128), channel_id=1, source_target_pairs={{0,32},{32,64},{64,96},{96,0},{1,33},{33,65},{65,97},{97,1},{2,34}... | collective-permute-start | bytes 200 | tf_op jit(solution)/shard_map/ppermute | solution.py:20
  12.8 3.5 copy-start.1
  12.8 82.6 %copy-start.23 = (s32[4]{0:T(128)S(1)}, s32[4]{0:T(128)}, u32[]{:S(2)}) copy-start(s32[4]{0:T(128)} %param.25) | copy-start | bytes 52
  12.8 83.2 %copy-start.25 = (s32[16]{0:T(128)S(1)}, s32[16]{0:T(128)}, u32[]{:S(2)}) copy-start(s32[16]{0:T(128)} %param.24) | copy-start | bytes 196
  12.8 85.3 %copy-start.7 = (bf16[512,128]{1,0:T(8,128)(2,1)S(1)}, bf16[512,128]{1,0:T(8,128)(2,1)}, u32[]{:S(2)}) copy-start(bf16[512,128]{1,0:T(8,128)(2,1)} %param.19) | copy-start | bytes 393220
  12.8 86.7 %copy-start.5 = (bf16[512,512]{1,0:T(8,128)(2,1)S(1)}, bf16[512,512]{1,0:T(8,128)(2,1)}, u32[]{:S(2)}) copy-start(bf16[512,512]{1,0:T(8,128)(2,1)} %param.17) | copy-start | bytes 1572868
  12.8 87.0 %copy-start.6 = (bf16[512,512]{1,0:T(8,128)(2,1)S(1)}, bf16[512,512]{1,0:T(8,128)(2,1)}, u32[]{:S(2)}) copy-start(bf16[512,512]{1,0:T(8,128)(2,1)} %param.18) | copy-start | bytes 1572868
  94.8 22.8 %copy-start.8 = (bf16[4,4096]{1,0:T(4,128)(2,1)}, bf16[4,4096]{1,0:T(4,128)(2,1)S(1)}, u32[]{:S(2)}) copy-start(bf16[4,4096]{1,0:T(4,128)(2,1)S(1)} %get-tuple-element.16) | copy-start | bytes 98308
  106.3 33.8 %copy-start.21 = (pred[128]{0:T(512)(128)(4,1)}, pred[128]{0:T(512)(128)(4,1)S(1)}, u32[]{:S(2)}) copy-start(pred[128]{0:T(512)(128)(4,1)S(1)} %broadcast_compare_fusion.2) | copy-start | bytes 388
  106.9 110.0 %all-to-all-start.2 = ((bf16[16,1,2]{2,1,0:T(2,128)(2,1)}), bf16[16,1,2]{2,1,0:T(2,128)(2,1)}, u32[]{:S(2)}, u32[]{:S(2)}) async-start(bf16[16,1,2]{2,1,0:T(2,128)(2,1)} %copy.72), calls=%async_computation.2 | async-start | bytes 16384 | tf_op jit(solution)/shard_map/all_to_all | solution.py:117
  119.5 20.6 %copy-start.12 = (bf16[128,512]{1,0:T(8,128)(2,1)S(1)}, bf16[128,512]{1,0:T(8,128)(2,1)}, u32[]{:S(2)}) copy-start(bf16[128,512]{1,0:T(8,128)(2,1)} %param.20) | copy-start | bytes 393220
  141.6 71.2 %copy-start.22 = (pred[128]{0:T(512)(128)(4,1)S(1)}, pred[128]{0:T(512)(128)(4,1)}, u32[]{:S(2)}) copy-start(pred[128]{0:T(512)(128)(4,1)} %copy-done.21) | copy-start | bytes 388
  141.6 75.4 %collective-permute-start = (bf16[16,2,32,512]{3,2,1,0:T(8,128)(2,1)S(1)}, bf16[16,2,32,512]{3,2,1,0:T(8,128)(2,1)}, u32[]{:S(2)}, u32[]{:S(2)}) collective-permute-start(bf16[16,2,32,512]{3,2,1,0:T(8,128)(2,1)S(1)} %bitcast.159), channel_id=1, source_target_pairs={{0,32},{32,64},{64,96},{96,0},{1,33},{33,65},{65,97},{97,1},{2,34}... | collective-permute-start | bytes 3145736 | tf_op jit(solution)/shard_map/ppermute | solution.py:20
  213.0 9.8 %copy-start.10 = (bf16[4,4096]{1,0:T(4,128)(2,1)S(1)}, bf16[4,4096]{1,0:T(4,128)(2,1)}, u32[]{:S(2)}) copy-start(bf16[4,4096]{1,0:T(4,128)(2,1)} %get-tuple-element.15) | copy-start | bytes 98308
  214.5 13.5 %copy-start.16 = (s32[1024]{0:T(1024)S(1)}, s32[1024]{0:T(1024)}, u32[]{:S(2)}) copy-start(s32[1024]{0:T(1024)} %iota_add_fusion) | copy-start | bytes 12292
  214.5 13.5 %copy-start.24 = (s32[4]{0:T(128)S(1)}, s32[4]{0:T(128)}, u32[]{:S(2)}) copy-start(s32[4]{0:T(128)} %param.26) | copy-start | bytes 52
  214.9 26.3 %collective-permute-start.1 = (bf16[16,2,32,512]{3,2,1,0:T(8,128)(2,1)S(1)}, bf16[16,2,32,512]{3,2,1,0:T(8,128)(2,1)}, u32[]{:S(2)}, u32[]{:S(2)}) collective-permute-start(bf16[16,2,32,512]{3,2,1,0:T(8,128)(2,1)S(1)} %bitcast.158), channel_id=1, source_target_pairs={{0,32},{32,64},{64,96},{96,0},{1,33},{33,65},{65,97},{97,1},{2,34}... | collective-permute-start | bytes 3145736 | tf_op jit(solution)/shard_map/ppermute | solution.py:20
  217.0 24.2 %all-to-all-start = ((bf16[16,2,32,512]{3,2,1,0:T(8,128)(2,1)}), bf16[16,2,32,512]{3,2,1,0:T(8,128)(2,1)S(1)}, u32[]{:S(2)}, u32[]{:S(2)}) async-start(bf16[16,2,32,512]{3,2,1,0:T(8,128)(2,1)} %collective-permute-done), calls=%async_computation | async-start | bytes 2097152 | tf_op jit(solution)/shard_map/all_to_all | solution.py:115
  227.0 20.3 %copy-start.9 = (bf16[4,4096]{1,0:T(4,128)(2,1)S(1)}, bf16[4,4096]{1,0:T(4,128)(2,1)}, u32[]{:S(2)}) copy-start(bf16[4,4096]{1,0:T(4,128)(2,1)} %copy-done.8) | copy-start | bytes 98308
  241.2 166.2 %all-to-all-start.1 = ((bf16[16,2,32,512]{3,2,1,0:T(8,128)(2,1)}), bf16[16,2,32,512]{3,2,1,0:T(8,128)(2,1)S(1)}, u32[]{:S(2)}, u32[]{:S(2)}) async-start(bf16[16,2,32,512]{3,2,1,0:T(8,128)(2,1)} %collective-permute-done.1), calls=%async_computation.1 | async-start | bytes 2097152 | tf_op jit(solution)/shard_map/all_to_all | solution.py:116
  246.5 244.2 %all-reduce.7.cloned.1.call-start = ((), (), s32[]{:S(2)}) async-start(), calls=%async_computation.6 | async-start | bytes 262144 | tf_op jit(solution)/shard_map/psum | solution.py:198
  246.8 2.6 copy-start.3
  246.8 2.5 copy-start.4
  246.8 78.7 %copy-start.14 = (f32[4,512]{1,0:T(4,128)S(1)}, f32[4,512]{1,0:T(4,128)}, u32[]{:S(2)}) copy-start(f32[4,512]{1,0:T(4,128)} %fusion.72) | copy-start | bytes 24580
  246.8 78.7 %copy-start.15 = (f32[4,512]{1,0:T(4,128)S(1)}, f32[4,512]{1,0:T(4,128)}, u32[]{:S(2)}) copy-start(f32[4,512]{1,0:T(4,128)} %fusion.80) | copy-start | bytes 24580
  247.3 151.3 %copy-start.13 = (bf16[128,512]{1,0:T(8,128)(2,1)S(1)}, bf16[128,512]{1,0:T(8,128)(2,1)}, u32[]{:S(2)}) copy-start(bf16[128,512]{1,0:T(8,128)(2,1)} %param.20) | copy-start | bytes 393220
  403.3 3.5 copy-start.2
  403.5 4.0 copy-start.19
  406.5 2.2 copy-start.17
  407.4 5.5 %copy-start.18 = (f32[4,4,8]{2,1,0:T(4,128)S(1)}, f32[4,4,8]{2,1,0:T(4,128)}, u32[]{:S(2)}) copy-start(f32[4,4,8]{2,1,0:T(4,128)} %get-tuple-element.11) | copy-start | bytes 1540
Sparse Core Ops, SparseCore 0:
  10.2 47.9 all-gather.5
  60.3 70.2 all-gather.3
  132.8 70.4 all-gather.7
  413.0 77.6 all-reduce.6
where the time goes:
time: 503 us; the launch traced here: 502 us
  blocking collectives  229 us (46%)
  waiting for transfers between devices  164 us (33%)
  matrix products  56.9 us (11%)
  starting transfers between devices  19.7 us (4%)
  between operations  14.2 us (3%)
  other arithmetic  12.1 us (2%)
  local copies, waits for them, and re-layouts  6.36 us (1%)
    psum x2, blocking collectives, on_device(): lax.psum((jnp.dot(step_hidden_states, query_matrix, preferred_element_typ...  148 us
    psum x1, waiting for transfers between devices, on_device(): lax.psum((block_total * factor, block_out * factor[..., None]), 'ctx')  77.7 us
    pmax x1, blocking collectives, on_device(): merged_max = lax.pmax(block_max, 'ctx')  74.9 us
    all_gather x1, waiting for transfers between devices, on_device(): lax.all_gather(value_matrix, 'ctx', axis=0, tiled=True)  60 us
    dot_general x3, matrix products, on_device(): jnp.dot(prefill_hidden_states, piece, preferred_element_type=jnp.float32)  25.4 us
    ppermute x3, waiting for transfers between devices, shifted(): lax.ppermute(value, axis, [(i, (i + by) % peers) for i in range(peers)])  13 us
    all_gather x1, waiting for transfers between devices, on_device(): lax.all_gather(key_matrix, 'ctx', axis=0, tiled=True)  11.1 us
  transfers between devices with their start and end apart: 10, of which 4 were waited for; matrix products, arithmetic and copies ran while one was open for 13% of the time, Pallas kernels for 0%

commit v1 on v0

v1 whole, which is shorter than its diff:
```python
import functools

import jax
import jax.numpy as jnp
from jax import lax
from jax.experimental import pallas as pl
from jax.experimental.pallas import tpu as pltpu
from jax.sharding import PartitionSpec as P

H = 64
KVH = 8
HD = 128
ADAPTER_RANK = 16
BLK = 32
STEPS = 2

ADAPTER_SCALE = 0.5
NEG_FLOOR = -1e30
INV_ROOT = HD ** (-0.5)

SIDE = 4
N_CTX = 16
SHARD = 512
UNITS = 9
HEADS = 4
ROWS = 512
SLOT_ROWS = 1024
PAIR = 64
RPG = 4
CTX_DEV = 1024
QROWS = 64
DBLOCKS = 48
PER = 3

MESH = pl.DeviceIdType.MESH
F32 = jnp.float32
BF16 = jnp.bfloat16


def pick_entry(table, wanted):
    places = jnp.arange(table.shape[0], dtype=jnp.int32)
    return jnp.sum(jnp.where(places == wanted, table, 0))


def wait_bytes(ref, sem):
    pltpu.make_async_copy(ref, ref, sem).wait()


def nt_dot(a, b):
    return lax.dot_general(a, b, (((1,), (1,)), ((), ())), preferred_element_type=F32)


def layer_kernel(
    info,
    xd,
    drow,
    x_hbm,
    wq_hbm,
    wk_hbm,
    wv_hbm,
    wd_hbm,
    uk_hbm,
    uv_hbm,
    kc_hbm,
    vc_hbm,
    pk_out,
    pv_out,
    att_out,
    x_v,
    w_v,
    wq_v,
    up_v,
    kc_v,
    vc_v,
    acc,
    dn,
    row,
    raw,
    place_m,
    drow_r,
    sendb,
    pages,
    part,
    rsr,
    ag,
    qp,
    tkv,
    pst,
    mgs,
    mgr,
    att,
    w_load,
    q_load,
    x_load,
    c_load,
    u_load,
    g_recv,
    g_send,
    row_send,
    row_recv,
    a_send,
    a_recv,
    small_send,
    small_recv,
    out_sem,
):
    s = lax.axis_index("section")
    c = lax.axis_index("ctx")
    t = lax.axis_index("tp")
    n_sec = lax.axis_size("section")
    y = c // SIDE
    z = lax.rem(c, SIDE)

    def chip(dy, dz):
        return lax.rem(y + dy + SIDE, SIDE) * SIDE + lax.rem(z + dz + SIDE, SIDE)

    def here(ctx):
        return (s, ctx, t)

    right = (lax.rem(s + 1, n_sec), c, t)
    left = (lax.rem(s + n_sec - 1, n_sec), c, t)
    partner = (s, c, 1 - t)

    barrier = pltpu.get_barrier_semaphore()

    @pl.loop(1, N_CTX)
    def _(j):
        pl.semaphore_signal(
            barrier, inc=1, device_id=here(lax.rem(c + j, N_CTX)), device_id_type=MESH
        )

    for peer in (left, right, partner):
        pl.semaphore_signal(barrier, inc=1, device_id=peer, device_id_type=MESH)

    mine = pl.ds(pl.multiple_of(c * SHARD, SHARD), SHARD)
    loads = [pltpu.make_async_copy(wd_hbm, w_v.at[0, mine], w_load.at[0])]
    for h in range(HEADS):
        cols = pl.ds(h * HD, HD)
        loads.append(
            pltpu.make_async_copy(wk_hbm.at[:, cols], w_v.at[1 + h, mine], w_load.at[1 + h])
        )
    for h in range(HEADS):
        cols = pl.ds(h * HD, HD)
        loads.append(
            pltpu.make_async_copy(wv_hbm.at[:, cols], w_v.at[5 + h, mine], w_load.at[5 + h])
        )
    for load in loads:
        load.start()
    q_copy = pltpu.make_async_copy(wq_hbm, wq_v, q_load)
    q_copy.start()
    ups = []
    for h in range(HEADS):
        cols = pl.ds(h * HD, HD)
        ups.append(pltpu.make_async_copy(uk_hbm.at[:, cols], up_v.at[h], u_load.at[h]))
        ups.append(pltpu.make_async_copy(uv_hbm.at[:, cols], up_v.at[4 + h], u_load.at[4 + h]))
    for load in ups:
        load.start()
    x_copy = pltpu.make_async_copy(x_hbm, x_v, x_load)
    x_copy.start()
    k_copy = pltpu.make_async_copy(kc_hbm, kc_v, c_load.at[0])
    v_copy = pltpu.make_async_copy(vc_hbm, vc_v, c_load.at[1])
    k_copy.start()
    v_copy.start()

    pl.semaphore_wait(barrier, N_CTX + 2)

    def send(src, dst, send_sem, recv_sem, device):
        pltpu.make_async_remote_copy(
            src_ref=src,
            dst_ref=dst,
            send_sem=send_sem,
            recv_sem=recv_sem,
            device_id=device,
            device_id_type=MESH,
        ).start()

    send(drow, drow_r, small_send.at[0], small_recv.at[0], right)

    for load in loads:
        load.wait()
    for load in ups:
        load.wait()

    def pass_on(u, stage, shard, first, count, ctx):
        rows = pl.ds(pl.multiple_of(shard * SHARD + first, 128), count)
        piece = w_v.at[u, rows]
        send(piece, piece, g_send.at[u], g_recv.at[u, stage], here(ctx))

    yp, ym, zp, zm = chip(1, 0), chip(-1, 0), chip(0, 1), chip(0, -1)
    A, B, A0, A1, B0, B1, ZERO = (
        (0, 256),
        (256, 256),
        (128, 128),
        (0, 128),
        (256, 128),
        (384, 128),
        (128, 256),
    )

    def stage1(u):
        for ctx in (yp, zp, ym, zm):
            pass_on(u, 0, c, 0, SHARD, ctx)

    def stage2(u):
        wait_bytes(w_v.at[u, pl.ds(0, 4 * SHARD)], g_recv.at[u, 0])
        pass_on(u, 1, ym, *ZERO, yp)
        pass_on(u, 1, yp, *A1, ym)
        pass_on(u, 1, yp, *B1, ym)
        pass_on(u, 1, zm, *ZERO, zp)
        pass_on(u, 1, zp, *A1, zm)
        pass_on(u, 1, zp, *B1, zm)
        for shard in (ym, yp):
            for ctx in (zp, zm):
                pass_on(u, 1, shard, *A, ctx)
        for shard in (zm, zp):
            for ctx in (yp, ym):
                pass_on(u, 1, shard, *B, ctx)

    def stage3(u):
        wait_bytes(w_v.at[u, pl.ds(0, 6 * SHARD)], g_recv.at[u, 1])
        yy, zz = chip(2, 0), chip(0, 2)
        for ctx in (zp, zm):
            pass_on(u, 2, yy, *A, ctx)
        for ctx in (yp, ym):
            pass_on(u, 2, zz, *B, ctx)
        for d in (-1, 1):
            pass_on(u, 2, chip(d, -1), *A0, zp)
            pass_on(u, 2, chip(d, 1), *A1, zm)
            pass_on(u, 2, chip(-1, d), *B0, yp)
            pass_on(u, 2, chip(1, d), *B1, ym)

    def stage4(u):
        wait_bytes(w_v.at[u, pl.ds(0, 4 * SHARD)], g_recv.at[u, 2])
        pass_on(u, 3, chip(2, -1), *A0, zp)
        pass_on(u, 3, chip(2, 1), *A1, zm)
        pass_on(u, 3, chip(-1, 2), *B0, yp)
        pass_on(u, 3, chip(1, 2), *B1, ym)

    def project(u):
        wait_bytes(w_v.at[u, pl.ds(0, SHARD)], g_recv.at[u, 3])

        @pl.when(u == 0)
        def _():
            x_copy.wait()

        acc[...] = jnp.zeros_like(acc)

        @pl.loop(0, 8)
        def _(i):
            part_k = pl.ds(pl.multiple_of(i * 1024, 1024), 1024)
            acc[...] += jnp.dot(x_v[:, part_k], w_v[u, part_k], preferred_element_type=F32)

        @pl.when(u == 0)
        def _():
            dn[t] = acc[...].astype(BF16)
            send(dn.at[t], dn.at[t], small_send.at[1], small_recv.at[1], partner)

        @pl.when(u == 1)
        def _():
            wait_bytes(dn.at[0], small_recv.at[1])

        @pl.when(u > 0)
        def _():
            n = u - 1
            column = lax.broadcasted_iota(jnp.int32, (ROWS, HD), 1) // ADAPTER_RANK
            picked = jnp.where(column == info[8], dn[n // HEADS].astype(F32), 0.0).astype(BF16)
            delta = jnp.dot(picked, up_v[n], preferred_element_type=F32)
            row[n] = (acc[...] + ADAPTER_SCALE * delta).astype(BF16)
            send(row.at[n], raw.at[n], row_send.at[n], row_recv.at[n], right)

    def exchange(n):
        @pl.loop(1, N_CTX)
        def _(j):
            ctx = lax.rem(c + j, N_CTX)
            theirs = pl.ds(pl.multiple_of(ctx * PAIR, PAIR), PAIR)
            ours = pl.ds(pl.multiple_of(c * PAIR, PAIR), PAIR)
            send(
                sendb.at[n, theirs], pages.at[n, ours], a_send.at[n], a_recv.at[n], here(ctx)
            )

        ours = pl.ds(pl.multiple_of(c * PAIR, PAIR), PAIR)
        pages[n, ours] = sendb[n, ours]

    def place(n):
        wait_bytes(raw.at[n], row_recv.at[n])

        @pl.loop(0, 4)
        def _(i):
            some = pl.ds(pl.multiple_of(i * 256, 256), 256)
            sendb[n, some] = jnp.dot(
                place_m[some], raw[n], preferred_element_type=F32
            ).astype(BF16)

        exchange(n)

    def page_flags():
        wait_bytes(drow_r, small_recv.at[0])

        @pl.loop(0, 4)
        def _(i):
            some = pl.ds(pl.multiple_of(i * 256, 256), 256)
            slot_row = lax.broadcasted_iota(jnp.int32, (256, ROWS), 0) + i * 256
            hit = slot_row == drow_r[0:1]
            place_m[some] = jnp.where(hit, 1.0, 0.0).astype(BF16)
            flag = jnp.max(jnp.where(hit, 1.0, 0.0), axis=1, keepdims=True)
            sendb[8, some] = jnp.broadcast_to(flag, (256, HD)).astype(BF16)

        exchange(8)

    def landed(n):
        wait_bytes(pages.at[n, pl.ds(0, SLOT_ROWS - PAIR)], a_recv.at[n])

    def write_out(n):
        cols = pl.ds(pl.multiple_of(lax.rem(n, HEADS) * HD, HD), HD)

        @pl.when(n < HEADS)
        def _():
            pltpu.make_async_copy(pages.at[n], pk_out.at[:, cols], out_sem.at[n]).start()

        @pl.when(n >= HEADS)
        def _():
            pltpu.make_async_copy(pages.at[n], pv_out.at[:, cols], out_sem.at[n]).start()

    def decode_project():
        q_copy.wait()

        def blocks(product, first):
            for i in range(product.shape[1] // HD):
                part[first + i] = product[:, i * HD : (i + 1) * HD]

        hidden = xd[...]
        part[DBLOCKS - 6 :] = jnp.zeros((6, 8, HD), F32)
        for i in range(8):
            piece = wq_v[:, i * 512 : (i + 1) * 512]
            blocks(jnp.dot(hidden, piece, preferred_element_type=F32), 4 * i)
        for u in range(1, UNITS):
            blocks(jnp.dot(hidden, w_v[u, mine], preferred_element_type=F32), 31 + u)
        part[40 + t] = jnp.dot(hidden, w_v[0, mine], preferred_element_type=F32)
        send(part.at[40 + t], part.at[40 + t], small_send.at[2], small_recv.at[2], partner)
        wait_bytes(part.at[0], small_recv.at[2])

        @pl.loop(1, N_CTX)
        def _(j):
            ctx = lax.rem(c + j, N_CTX)
            send(
                part.at[pl.ds(ctx * PER, PER)],
                rsr.at[c],
                small_send.at[3],
                small_recv.at[3],
                here(ctx),
            )

        rsr[c] = part[pl.ds(c * PER, PER)]

    def decode_sum():
        wait_bytes(rsr.at[pl.ds(0, N_CTX - 1)], small_recv.at[3])
        ag[pl.ds(c * PER, PER)] = jnp.sum(rsr[...], axis=0)

        @pl.loop(1, N_CTX)
        def _(j):
            ctx = lax.rem(c + j, N_CTX)
            piece = ag.at[pl.ds(c * PER, PER)]
            send(piece, piece, small_send.at[4], small_recv.at[4], here(ctx))

    def decode_rows():
        wait_bytes(ag.at[pl.ds(0, (N_CTX - 1) * PER)], small_recv.at[4])
        to = lax.broadcasted_iota(jnp.int32, (QROWS, QROWS), 0)
        at = lax.broadcasted_iota(jnp.int32, (QROWS, QROWS), 1)
        source = lax.rem(to, 8) * 8 + lax.rem(to // 8, STEPS) * RPG + to // 16
        perm = jnp.where(at == source, 1.0, 0.0).astype(BF16)
        for k in range(HEADS):
            queries = ag[8 * k : 8 * k + 8].reshape(QROWS, HD).astype(BF16)
            qp[k] = jnp.dot(perm, queries, preferred_element_type=F32).astype(BF16)
        lane = lax.broadcasted_iota(jnp.int32, (8, HD), 1) // ADAPTER_RANK
        who = lax.rem(lax.broadcasted_iota(jnp.int32, (8, HD), 0), RPG)
        adapter = jnp.zeros((8, HD), jnp.int32)
        for b in range(RPG):
            adapter = jnp.where(who == b, info[9 + b], adapter)
        for kind in range(2):
            down = ag[40 + kind].astype(BF16).astype(F32)
            picked = jnp.where(lane == adapter, down, 0.0).astype(BF16)
            for k in range(HEADS):
                n = 4 * kind + k
                delta = jnp.dot(picked, up_v[n], preferred_element_type=F32)
                tkv[n] = (ag[32 + n] + ADAPTER_SCALE * delta).astype(BF16).astype(F32)

    def cache_block(b):
        @pl.when(b == 0)
        def _():
            k_copy.wait()
            v_copy.wait()

        left_len = info[b]
        live = lax.broadcasted_iota(jnp.int32, (16, CTX_DEV), 1) < left_len
        rows = pl.ds(pl.multiple_of(b * 16, 16), 16)
        for k in range(HEADS):
            cols = slice(k * HD, (k + 1) * HD)
            scores = nt_dot(qp[k, rows], kc_v[b, :, cols]) * INV_ROOT
            block_max = jnp.max(jnp.where(live, scores, NEG_FLOOR), axis=1, keepdims=True)
            weights = jnp.where(live, jnp.exp(scores - block_max), 0.0).astype(BF16)
            total = jnp.sum(weights.astype(F32), axis=1, keepdims=True)
            pst[0, k, rows] = jnp.broadcast_to(block_max, (16, HD))
            pst[1, k, rows] = jnp.broadcast_to(total, (16, HD))
            pst[2, k, rows] = jnp.dot(weights, vc_v[b, :, cols], preferred_element_type=F32)

    @pl.loop(0, UNITS + 6)
    def _(i):
        @pl.when(i < UNITS)
        def _():
            stage1(i)

        @pl.when(i == 0)
        def _():
            decode_project()

        @pl.when((i >= 3) & (i < UNITS + 3))
        def _():
            stage4(i - 3)

        @pl.when((i >= 2) & (i < UNITS + 2))
        def _():
            stage3(i - 2)

        @pl.when((i >= 1) & (i < UNITS + 1))
        def _():
            stage2(i - 1)

        @pl.when(i == 1)
        def _():
            decode_sum()
            page_flags()

        @pl.when(i == 2)
        def _():
            decode_rows()

        @pl.when((i >= 3) & (i < 3 + RPG))
        def _():
            cache_block(i - 3)

        @pl.when((i >= 4) & (i < UNITS + 4))
        def _():
            project(i - 4)

        @pl.when((i >= 6) & (i < UNITS + 5))
        def _():
            place(i - 6)

        @pl.when(i >= 7)
        def _():
            landed(i - 7)
            write_out(i - 7)

    landed(8)

    live = nt_dot(jnp.ones((16, HD), BF16), pages[8]) > 0.5
    which = lax.broadcasted_iota(jnp.int32, (QROWS, 8), 0)
    other = lax.broadcasted_iota(jnp.int32, (QROWS, 8), 1)
    tok_live = (
        (lax.rem(other, RPG) == which // 16)
        & (other // RPG <= lax.rem(which // 8, STEPS))
        & (c == 0)
    )
    lane = lax.broadcasted_iota(jnp.int32, (16, HD), 1)
    for k in range(HEADS):
        query = jnp.zeros((16, HD), F32)
        for b in range(RPG):
            query = jnp.where(info[4 + b] == 1, qp[k, b * 16 : b * 16 + 16].astype(F32), query)
        scores = nt_dot(query.astype(BF16), pages[k]) * INV_ROOT
        p_max = jnp.max(jnp.where(live, scores, NEG_FLOOR), axis=1, keepdims=True)
        weights = jnp.where(live, jnp.exp(scores - p_max), 0.0).astype(BF16)
        p_total = jnp.sum(weights.astype(F32), axis=1, keepdims=True)
        p_out = jnp.dot(weights, pages[4 + k], preferred_element_type=F32)
        tok = nt_dot(qp[k], tkv[k].astype(BF16)) * INV_ROOT
        tok_max = jnp.max(jnp.where(tok_live, tok, NEG_FLOOR), axis=1, keepdims=True)
        tok_w = jnp.where(tok_live, jnp.exp(tok - tok_max), 0.0)
        tok_total = jnp.sum(tok_w, axis=1, keepdims=True)
        tok_out = jnp.zeros((QROWS, HD), F32)
        for i in range(8):
            tok_out = tok_out + tok_w[:, i : i + 1] * tkv[4 + k, i : i + 1]
        for b in range(RPG):
            rows = slice(b * 16, b * 16 + 16)
            wanted = info[4 + b] == 1
            pm = jnp.where(wanted, p_max, NEG_FLOOR)
            pt = jnp.where(wanted, p_total, 0.0)
            po = jnp.where(wanted, p_out, 0.0)
            cm = pst[0, k, rows]
            tm = tok_max[rows]
            top = jnp.maximum(jnp.maximum(cm, pm), tm)
            c_scale, p_scale, t_scale = jnp.exp(cm - top), jnp.exp(pm - top), jnp.exp(tm - top)
            total = c_scale * pst[1, k, rows] + p_scale * pt + t_scale * tok_total[rows]
            mgs[k * 4 + b, 0] = (
                c_scale * pst[2, k, rows] + p_scale * po + t_scale * tok_out[rows]
            )
            mgs[k * 4 + b, 1] = jnp.where(lane < 64, top, total)

    @pl.loop(1, N_CTX)
    def _(j):
        ctx = lax.rem(c + j, N_CTX)
        send(mgs.at[ctx], mgr.at[c], small_send.at[5], small_recv.at[5], here(ctx))

    mgr[c] = mgs[c]
    wait_bytes(mgr.at[pl.ds(0, N_CTX - 1)], small_recv.at[5])
    stats = mgr[:, 1]
    tops, totals = stats[:, :, 0:1], stats[:, :, 64:65]
    scale = jnp.exp(tops - jnp.max(tops, axis=0, keepdims=True))
    numer = jnp.sum(scale * mgr[:, 0], axis=0)
    denom = jnp.sum(scale * totals, axis=0)
    att[c] = (numer / denom).astype(BF16)

    @pl.loop(1, N_CTX)
    def _(j):
        ctx = lax.rem(c + j, N_CTX)
        send(att.at[c], att.at[c], small_send.at[6], small_recv.at[6], here(ctx))

    wait_bytes(att.at[pl.ds(0, N_CTX - 1)], small_recv.at[6])
    att_out[...] = att[...]

    @pl.loop(0, UNITS)
    def _(u):
        wait_bytes(w_v.at[u, pl.ds(0, 15 * SHARD)], g_send.at[u])
        wait_bytes(sendb.at[u, pl.ds(0, SLOT_ROWS - PAIR)], a_send.at[u])

    @pl.loop(0, 2 * HEADS)
    def _(n):
        wait_bytes(row.at[n], row_send.at[n])
        wait_bytes(pages.at[n], out_sem.at[n])

    wait_bytes(drow, small_send.at[0])
    wait_bytes(dn.at[0], small_send.at[1])
    wait_bytes(part.at[0], small_send.at[2])
    wait_bytes(rsr.at[pl.ds(0, N_CTX - 1)], small_send.at[3])
    wait_bytes(ag.at[pl.ds(0, (N_CTX - 1) * PER)], small_send.at[4])
    wait_bytes(mgr.at[pl.ds(0, N_CTX - 1)], small_send.at[5])
    wait_bytes(att.at[pl.ds(0, N_CTX - 1)], small_send.at[6])


def on_device(
    prefill_hidden_states,
    decode_hidden_states,
    query_matrix,
    key_matrix,
    value_matrix,
    adapter_down_maps,
    key_adapter_up_maps,
    value_adapter_up_maps,
    request_key_cache,
    request_value_cache,
    request_adapter_index,
    prefill_request_target,
    request_context_length,
    page_owner_index,
):
    n_section = lax.axis_size("section")
    section_at = lax.axis_index("section")
    ctx_at = lax.axis_index("ctx")
    span_request = pick_entry(prefill_request_target, section_at)
    span_adapter = pick_entry(request_adapter_index, span_request)
    page_request = pick_entry(prefill_request_target, (section_at + n_section - 1) % n_section)
    local_ids = section_at * RPG + jnp.arange(RPG, dtype=jnp.int32)
    batch_ids = jnp.arange(request_adapter_index.shape[0], dtype=jnp.int32)
    adapters = jnp.sum(
        jnp.where(local_ids[:, None] == batch_ids[None, :], request_adapter_index[None, :], 0),
        axis=1,
    )
    info = jnp.concatenate(
        [
            request_context_length - ctx_at * CTX_DEV,
            (local_ids == page_request).astype(jnp.int32),
            span_adapter[None],
            adapters,
            jnp.zeros((3,), jnp.int32),
        ]
    ).astype(jnp.int32)
    owners = page_owner_index[:, 0]
    order = jnp.arange(owners.shape[0], dtype=jnp.int32)
    earlier = (owners[None, :] == owners[:, None]) & (order[None, :] < order[:, None])
    slot_of = owners * 2 + jnp.sum(earlier, axis=1).astype(jnp.int32)
    drow = (slot_of[:, None] * BLK + jnp.arange(BLK, dtype=jnp.int32)[None, :]).reshape(1, ROWS)
    drow = jnp.broadcast_to(drow, (8, ROWS))
    decode_rows = decode_hidden_states.reshape(STEPS * RPG, SHARD)

    hbm = pl.BlockSpec(memory_space=pl.ANY)
    vmem = pl.BlockSpec(memory_space=pltpu.VMEM)
    smem = pl.BlockSpec(memory_space=pltpu.SMEM)
    dma = pltpu.SemaphoreType.DMA
    page_keys, page_values, attended = pl.pallas_call(
        layer_kernel,
        out_shape=(
            jax.ShapeDtypeStruct((SLOT_ROWS, HEADS * HD), BF16),
            jax.ShapeDtypeStruct((SLOT_ROWS, HEADS * HD), BF16),
            jax.ShapeDtypeStruct((N_CTX, 16, HD), BF16),
        ),
        in_specs=[smem, vmem, vmem] + [hbm] * 9,
        out_specs=(hbm, hbm, vmem),
        scratch_shapes=[
            pltpu.VMEM((ROWS, 8192), BF16),
            pltpu.VMEM((UNITS, 8192, HD), BF16),
            pltpu.VMEM((SHARD, 4096), BF16),
            pltpu.VMEM((8, HD, HD), BF16),
            pltpu.VMEM((RPG, CTX_DEV, HEADS * HD), BF16),
            pltpu.VMEM((RPG, CTX_DEV, HEADS * HD), BF16),
            pltpu.VMEM((ROWS, HD), F32),
            pltpu.VMEM((2, ROWS, HD), BF16),
            pltpu.VMEM((8, ROWS, HD), BF16),
            pltpu.VMEM((8, ROWS, HD), BF16),
            pltpu.VMEM((SLOT_ROWS, ROWS), BF16),
            pltpu.VMEM((8, ROWS), jnp.int32),
            pltpu.VMEM((9, SLOT_ROWS, HD), BF16),
            pltpu.VMEM((9, SLOT_ROWS, HD), BF16),
            pltpu.VMEM((DBLOCKS, 8, HD), F32),
            pltpu.VMEM((N_CTX, PER, 8, HD), F32),
            pltpu.VMEM((DBLOCKS, 8, HD), F32),
            pltpu.VMEM((HEADS, QROWS, HD), BF16),
            pltpu.VMEM((8, 8, HD), F32),
            pltpu.VMEM((3, HEADS, QROWS, HD), F32),
            pltpu.VMEM((N_CTX, 2, 16, HD), F32),
            pltpu.VMEM((N_CTX, 2, 16, HD), F32),
            pltpu.VMEM((N_CTX, 16, HD), BF16),
            dma((UNITS,)),
            dma,
            dma,
            dma((2,)),
            dma((8,)),
            dma((UNITS, 4)),
            dma((UNITS,)),
            dma((8,)),
            dma((8,)),
            dma((9,)),
            dma((9,)),
            dma((7,)),
            dma((7,)),
            dma((8,)),
        ],
        compiler_params=pltpu.CompilerParams(
            collective_id=0, has_side_effects=True, vmem_limit_bytes=58 * 1024 * 1024
        ),
        cost_estimate=pl.CostEstimate(
            flops=12_000_000_000, bytes_accessed=30_000_000, transcendentals=600_000
        ),
    )(
        info,
        decode_rows,
        drow,
        prefill_hidden_states,
        query_matrix,
        key_matrix,
        value_matrix,
        adapter_down_maps,
        key_adapter_up_maps,
        value_adapter_up_maps,
        request_key_cache,
        request_value_cache,
    )
    page_shape = (SLOT_ROWS // BLK, BLK, HEADS * HD)
    attended = attended.reshape(HEADS, RPG, STEPS, H // KVH, HD)
    attended = jnp.transpose(attended, (2, 1, 0, 3, 4)).reshape(STEPS, RPG, HEADS * 8 * HD)
    return (page_keys.reshape(page_shape), page_values.reshape(page_shape), attended)


def solution(mesh):
    return jax.shard_map(
        on_device,
        mesh=mesh,
        in_specs=(
            P(("section", "ctx"), None),
            P(None, "section", "ctx"),
            P("ctx", "tp"),
            P("ctx", "tp"),
            P("ctx", "tp"),
            P("ctx", "tp"),
            P(None, "tp"),
            P(None, "tp"),
            P("section", "ctx", "tp"),
            P("section", "ctx", "tp"),
            P(),
            P(),
            P("section"),
            P(("section", "ctx"), None),
        ),
        out_specs=(
            P(("section", "ctx"), None, "tp"),
            P(("section", "ctx"), None, "tp"),
            P(None, "section", "tp"),
        ),
        check_vma=False,
    )
```

time: 503 us -> 176 us (0.35)
  blocking collectives: 229 us -> 0 us
  waiting for transfers between devices: 164 us -> 0 us
  Pallas kernels: 0 us -> 159 us
  matrix products: 56.9 us -> 0 us
  starting transfers between devices: 19.7 us -> 0 us
  between operations: 14.2 us -> 0.68 us
  other arithmetic: 12.1 us -> 7.03 us
    pallas_call x0 -> x1, Pallas kernels: none -> 159 us  [on_device(): pl.pallas_call(layer_kernel, out_shape=(jax.ShapeDtypeStruct((SLOT_ROWS,...]
    psum x2 -> x0, blocking collectives: 148 us -> none  [on_device(): lax.psum((jnp.dot(step_hidden_states, query_matrix, preferred_element_typ...]
    psum x1 -> x0, waiting for transfers between devices: 77.7 us -> none  [on_device(): lax.psum((block_total * factor, block_out * factor[..., None]), 'ctx')]
    pmax x1 -> x0, blocking collectives: 74.9 us -> none  [on_device(): merged_max = lax.pmax(block_max, 'ctx')]
    all_gather x3 -> x0, waiting for transfers between devices: 71.1 us -> none  [the longest x1 60 us: on_device(): lax.all_gather(value_matrix, 'ctx', axis=0, tiled=True)]
    dot_general x30 -> x0, matrix products: 56.9 us -> none  [the longest x3 25.4 us: on_device(): jnp.dot(prefill_hidden_states, piece, preferred_element_type=jnp.float32)]
    all_to_all x3 -> x0, starting transfers between devices: 14.6 us -> none  [the longest x1 5.29 us: on_device(): lax.all_to_all(moved_keys, 'ctx', split_axis=0, concat_axis=0, tiled=True)]
    ppermute x3 -> x0, waiting for transfers between devices: 13 us -> none  [shifted(): lax.ppermute(value, axis, [(i, (i + by) % peers) for i in range(peers)])]
  transfers between devices with their start and end apart: 10 -> 0, of which waited for: 4 -> 0; matrix products, arithmetic and copies ran while one was open for 13% -> 0% of each run, Pallas kernels for 0% -> 0%
where the time goes in v1:
time: 176 us
  Pallas kernels  159 us (90%)
  local copies, waits for them, and re-layouts  9.4 us (5%)
  other arithmetic  7.03 us (4%)
    pallas_call x1, Pallas kernels, on_device(): pl.pallas_call(layer_kernel, out_shape=(jax.ShapeDtypeStruct((SLOT_ROWS,...  159 us
    unnamed x2, local copies, waits for them, and re-layouts  4.61 us

profile of v1, /device:TPU:0, one launch (start us, length us, event | category | flops | bytes accessed | tf_op | source)
XLA Modules:
  0.0 175.8 jit_solution(17349685485780872864)
XLA Ops:
  0.6 0.7 broadcast_subtract_fusion
  1.3 1.3 fusion.2
  2.6 1.9 %fusion.3 = s32[]{:T(128)} fusion(s32[16]{0:T(128)} %param.24, s32[]{:T(128)} %get-tuple-element.9), kind=kLoop, calls=%fused_computation.12 | loop fusion | flops 47 | bytes 72 | tf_op jit(solution)/shard_map/reduce_sum | solution.py:42
  4.5 0.6 compare_convert_fusion
  5.2 0.8 select_reduce_fusion
  6.0 0.9 convert_reduce_fusion
  7.0 0.7 fusion.5
  7.6 1.3 concatenate.3.info
  8.9 0.1 iota_add_fusion
  9.0 0.1 add.52
  9.1 1.3 reshape.44.xd
  10.4 0.6 broadcast_in_dim.41.drow
  11.0 158.7 %shard_map.157 = (bf16[1024,512]{1,0:T(8,128)(2,1)}, bf16[1024,512]{1,0:T(8,128)(2,1)}, bf16[16,16,128]{2,1,0:T(8,128)(2,1)}) custom-call(s32[16]{0:T(128)} %concatenate.3.info, bf16[8,512]{1,0:T(8,128)(2,1)} %reshape.44.xd, s32[8,512]{1,0:T(8,128)} %broadcast_in_dim.41.drow, bf16[512,8192]{1,0:T(8,128)(2,1)} %x_hbm.1, bf16[512,4096]{1,0:T(8,128)(2,1)} %wq_hbm.1, ...), custom_call_target="tpu_custom_call" | custom-call | flops 12000000000 | bytes 30000000 | tf_op jit(solution)/shard_map/pallas_call | solution.py:587
  169.7 0.9 copy.18
  170.6 0.7 reshape.48
  171.2 2.3 %copy.21 = bf16[32,32,512]{2,1,0:T(8,128)(2,1)} copy(bf16[32,32,512]{2,1,0:T(8,128)(2,1)} %bitcast.18) | data formatting | bytes 2097152
  173.5 2.3 %copy.22 = bf16[32,32,512]{2,1,0:T(8,128)(2,1)} copy(bf16[32,32,512]{2,1,0:T(8,128)(2,1)} %bitcast.17) | data formatting | bytes 2097152
  (2 shorter events, 0.0 us)

commit v2 on v1

--- a/solution.py
+++ b/solution.py
@@ -15,13 +15,15 @@
 STEPS = 2
 
 ADAPTER_SCALE = 0.5
+CUT = 128
 NEG_FLOOR = -1e30
 INV_ROOT = HD ** (-0.5)
 
 SIDE = 4
 N_CTX = 16
 SHARD = 512
-UNITS = 9
+UNITS = 5
+BLOCKS = 8
 HEADS = 4
 ROWS = 512
 SLOT_ROWS = 1024
@@ -37,11 +39,6 @@
 BF16 = jnp.bfloat16
 
 
-def pick_entry(table, wanted):
-    places = jnp.arange(table.shape[0], dtype=jnp.int32)
-    return jnp.sum(jnp.where(places == wanted, table, 0))
-
-
 def wait_bytes(ref, sem):
     pltpu.make_async_copy(ref, ref, sem).wait()
 
@@ -51,9 +48,11 @@
 
 
 def layer_kernel(
-    info,
+    adapter_of,
+    target_of,
+    length_of,
+    owner_of,
     xd,
-    drow,
     x_hbm,
     wq_hbm,
     wk_hbm,
@@ -69,6 +68,9 @@
     x_v,
     w_v,
     wq_v,
+    wd_v,
+    dt_v,
+    hid,
     up_v,
     kc_v,
     vc_v,
@@ -77,6 +79,7 @@
     row,
     raw,
     place_m,
+    drow,
     drow_r,
     sendb,
     pages,
@@ -96,6 +99,10 @@
     u_load,
     g_recv,
     g_send,
+    x_recv,
+    x_send,
+    f_recv,
+    f_send,
     row_send,
     row_recv,
     a_send,
@@ -120,6 +127,9 @@
     right = (lax.rem(s + 1, n_sec), c, t)
     left = (lax.rem(s + n_sec - 1, n_sec), c, t)
     partner = (s, c, 1 - t)
+    s_left = lax.rem(s + n_sec - 1, n_sec)
+    s_right = lax.rem(s + 1, n_sec)
+    s_far = lax.rem(s + 2, n_sec)
 
     barrier = pltpu.get_barrier_semaphore()
 
@@ -133,18 +143,15 @@
         pl.semaphore_signal(barrier, inc=1, device_id=peer, device_id_type=MESH)
 
     mine = pl.ds(pl.multiple_of(c * SHARD, SHARD), SHARD)
-    loads = [pltpu.make_async_copy(wd_hbm, w_v.at[0, mine], w_load.at[0])]
-    for h in range(HEADS):
-        cols = pl.ds(h * HD, HD)
-        loads.append(
-            pltpu.make_async_copy(wk_hbm.at[:, cols], w_v.at[1 + h, mine], w_load.at[1 + h])
+    shard_loads = []
+    for n, hbm in enumerate([wk_hbm] * HEADS + [wv_hbm] * HEADS):
+        cols = pl.ds(n % HEADS * HD, HD)
+        shard_loads.append(
+            pltpu.make_async_copy(hbm.at[:, cols], w_v.at[n, mine], w_load.at[n])
         )
-    for h in range(HEADS):
-        cols = pl.ds(h * HD, HD)
-        loads.append(
-            pltpu.make_async_copy(wv_hbm.at[:, cols], w_v.at[5 + h, mine], w_load.at[5 + h])
-        )
-    for load in loads:
+    down_load = pltpu.make_async_copy(wd_hbm, wd_v, w_load.at[8])
+    down_load.start()
+    for load in shard_loads:
         load.start()
     q_copy = pltpu.make_async_copy(wq_hbm, wq_v, q_load)
     q_copy.start()
@@ -174,17 +181,19 @@
             device_id_type=MESH,
         ).start()
 
-    send(drow, drow_r, small_send.at[0], small_recv.at[0], right)
-
-    for load in loads:
-        load.wait()
-    for load in ups:
+    for load in shard_loads:
         load.wait()
 
     def pass_on(u, stage, shard, first, count, ctx):
         rows = pl.ds(pl.multiple_of(shard * SHARD + first, 128), count)
-        piece = w_v.at[u, rows]
+        piece = w_v.at[block_of(u), rows]
         send(piece, piece, g_send.at[u], g_recv.at[u, stage], here(ctx))
+
+    def block_of(u):
+        return jnp.where(u == 0, HEADS + s, u - 1)
+
+    def arrived(u, stage, shards):
+        wait_bytes(w_v.at[block_of(u), pl.ds(0, shards * SHARD)], g_recv.at[u, stage])
 
     yp, ym, zp, zm = chip(1, 0), chip(-1, 0), chip(0, 1), chip(0, -1)
     A, B, A0, A1, B0, B1, ZERO = (
@@ -202,7 +211,7 @@
             pass_on(u, 0, c, 0, SHARD, ctx)
 
     def stage2(u):
-        wait_bytes(w_v.at[u, pl.ds(0, 4 * SHARD)], g_recv.at[u, 0])
+        arrived(u, 0, 4)
         pass_on(u, 1, ym, *ZERO, yp)
         pass_on(u, 1, yp, *A1, ym)
         pass_on(u, 1, yp, *B1, ym)
@@ -217,7 +226,7 @@
                 pass_on(u, 1, shard, *B, ctx)
 
     def stage3(u):
-        wait_bytes(w_v.at[u, pl.ds(0, 6 * SHARD)], g_recv.at[u, 1])
+        arrived(u, 1, 6)
         yy, zz = chip(2, 0), chip(0, 2)
         for ctx in (zp, zm):
             pass_on(u, 2, yy, *A, ctx)
@@ -230,43 +239,101 @@
             pass_on(u, 2, chip(1, d), *B1, ym)
 
     def stage4(u):
-        wait_bytes(w_v.at[u, pl.ds(0, 4 * SHARD)], g_recv.at[u, 2])
+        arrived(u, 2, 4)
         pass_on(u, 3, chip(2, -1), *A0, zp)
         pass_on(u, 3, chip(2, 1), *A1, zm)
         pass_on(u, 3, chip(-1, 2), *B0, yp)
         pass_on(u, 3, chip(1, 2), *B1, ym)
 
-    def project(u):
-        wait_bytes(w_v.at[u, pl.ds(0, SHARD)], g_recv.at[u, 3])
-
-        @pl.when(u == 0)
-        def _():
-            x_copy.wait()
-
+    GROUPS = (
+        (ym, yp, zm, zp),
+        (chip(-1, -1), chip(-1, 1), chip(1, -1), chip(1, 1), chip(2, 0), chip(0, 2)),
+        (chip(-1, 2), chip(1, 2), chip(2, -1), chip(2, 1)),
+        (chip(2, 2),),
+    )
+
+    def across(group):
+        for shard in GROUPS[group]:
+            rows = pl.ds(pl.multiple_of(shard * SHARD, SHARD), SHARD)
+            piece = w_v.at[HEADS + s, rows]
+            send(piece, piece, x_send.at[0], x_recv.at[0, group], right)
+            send(piece, piece, x_send.at[1], x_recv.at[1, group], left)
+
+    def across_again(group):
+        count = len(GROUPS[group])
+        wait_bytes(w_v.at[HEADS + s_left, pl.ds(0, count * SHARD)], x_recv.at[0, group])
+        wait_bytes(w_v.at[HEADS + s_right, pl.ds(0, count * SHARD)], x_recv.at[1, group])
+        for shard in GROUPS[group]:
+            rows = pl.ds(pl.multiple_of(shard * SHARD, SHARD), CUT)
+            piece = w_v.at[HEADS + s_left, rows]
+            send(piece, piece, f_send.at[0], f_recv.at[0], right)
+            rows = pl.ds(pl.multiple_of(shard * SHARD + CUT, 128), SHARD - CUT)
+            piece = w_v.at[HEADS + s_right, rows]
+            send(piece, piece, f_send.at[1], f_recv.at[1], left)
+
+    span_request = target_of[s]
+    span_adapter = jnp.int32(0)
+    for b in range(N_CTX):
+        span_adapter = jnp.where(span_request == b, adapter_of[b], span_adapter)
+    pick_row = lax.broadcasted_iota(jnp.int32, (ADAPTER_RANK, HD), 0)
+    pick_col = lax.broadcasted_iota(jnp.int32, (ADAPTER_RANK, HD), 1)
+    pick = jnp.where(pick_col == span_adapter * ADAPTER_RANK + pick_row, 1.0, 0.0).astype(BF16)
+
+    def down_rows():
+        down_load.wait()
+        own = pl.ds(pl.multiple_of(c * SHARD, SHARD), SHARD)
+        dt_v[:, own] = nt_dot(pick, wd_v[...]).astype(BF16)
+
+        @pl.loop(1, N_CTX)
+        def _(j):
+            piece = dt_v.at[:, own]
+            ctx = lax.rem(c + j, N_CTX)
+            send(piece, piece, small_send.at[7], small_recv.at[7], here(ctx))
+
+    def project_down():
+        x_copy.wait()
+        wait_bytes(dt_v.at[:, pl.ds(0, (N_CTX - 1) * SHARD)], small_recv.at[7])
         acc[...] = jnp.zeros_like(acc)
 
         @pl.loop(0, 8)
         def _(i):
             part_k = pl.ds(pl.multiple_of(i * 1024, 1024), 1024)
-            acc[...] += jnp.dot(x_v[:, part_k], w_v[u, part_k], preferred_element_type=F32)
-
-        @pl.when(u == 0)
-        def _():
-            dn[t] = acc[...].astype(BF16)
-            send(dn.at[t], dn.at[t], small_send.at[1], small_recv.at[1], partner)
-
-        @pl.when(u == 1)
+            acc[:, 0:ADAPTER_RANK] += nt_dot(x_v[:, part_k], dt_v[:, part_k])
+
+        down = acc[:, 0:ADAPTER_RANK].astype(BF16)
+        dn[t] = jnp.dot(down, pick, preferred_element_type=F32).astype(BF16)
+        send(dn.at[t], dn.at[t], small_send.at[1], small_recv.at[1], partner)
+
+    def nth(p, sec):
+        far = jnp.where(p == 5, sec + n_sec - 1, jnp.where(p == 6, sec + 1, sec + 2))
+        value = HEADS + jnp.where(p == 0, sec, lax.rem(far, n_sec))
+        return jnp.where((p >= 1) & (p <= HEADS), p - 1, value)
+
+    def project(p):
+        n = nth(p, s)
+
+        @pl.when((p >= 1) & (p < UNITS))
+        def _():
+            arrived(p, 3, 1)
+
+        @pl.when(p == 0)
         def _():
             wait_bytes(dn.at[0], small_recv.at[1])
 
-        @pl.when(u > 0)
-        def _():
-            n = u - 1
-            column = lax.broadcasted_iota(jnp.int32, (ROWS, HD), 1) // ADAPTER_RANK
-            picked = jnp.where(column == info[8], dn[n // HEADS].astype(F32), 0.0).astype(BF16)
-            delta = jnp.dot(picked, up_v[n], preferred_element_type=F32)
-            row[n] = (acc[...] + ADAPTER_SCALE * delta).astype(BF16)
-            send(row.at[n], raw.at[n], row_send.at[n], row_recv.at[n], right)
+        @pl.when(p == BLOCKS - 1)
+        def _():
+            wait_bytes(w_v.at[n, pl.ds(0, 15 * CUT)], f_recv.at[0])
+            wait_bytes(w_v.at[n, pl.ds(0, 15 * (SHARD - CUT))], f_recv.at[1])
+
+        acc[...] = jnp.dot(dn[n // HEADS], up_v[n], preferred_element_type=F32) * ADAPTER_SCALE
+
+        @pl.loop(0, 8)
+        def _(i):
+            part_k = pl.ds(pl.multiple_of(i * 1024, 1024), 1024)
+            acc[...] += jnp.dot(x_v[:, part_k], w_v[n, part_k], preferred_element_type=F32)
+
+        row[n] = acc[...].astype(BF16)
+        send(row.at[n], raw.at[n], row_send.at[n], row_recv.at[n], right)
 
     def exchange(n):
         @pl.loop(1, N_CTX)
@@ -293,6 +360,18 @@
 
         exchange(n)
 
+    def page_rows():
+        owners = [owner_of[i, 0] for i in range(16)]
+        lane = lax.broadcasted_iota(jnp.int32, (8, ROWS), 1)
+        rows = jnp.zeros((8, ROWS), jnp.int32)
+        for i in range(16):
+            slot = owners[i] * 2
+            for j in range(i):
+                slot = slot + jnp.where(owners[j] == owners[i], 1, 0)
+            rows = jnp.where(lane // BLK == i, slot * BLK + lax.rem(lane, BLK), rows)
+        drow[...] = rows
+        send(drow, drow_r, small_send.at[0], small_recv.at[0], right)
+
     def page_flags():
         wait_bytes(drow_r, small_recv.at[0])
 
@@ -328,14 +407,16 @@
             for i in range(product.shape[1] // HD):
                 part[first + i] = product[:, i * HD : (i + 1) * HD]
 
-        hidden = xd[...]
+        hid[0:4] = xd[0].astype(F32)
+        hid[4:8] = xd[1].astype(F32)
+        hidden = hid[...].astype(BF16)
         part[DBLOCKS - 6 :] = jnp.zeros((6, 8, HD), F32)
         for i in range(8):
             piece = wq_v[:, i * 512 : (i + 1) * 512]
             blocks(jnp.dot(hidden, piece, preferred_element_type=F32), 4 * i)
-        for u in range(1, UNITS):
-            blocks(jnp.dot(hidden, w_v[u, mine], preferred_element_type=F32), 31 + u)
-        part[40 + t] = jnp.dot(hidden, w_v[0, mine], preferred_element_type=F32)
+        for n in range(BLOCKS):
+            blocks(jnp.dot(hidden, w_v[n, mine], preferred_element_type=F32), 32 + n)
+        part[40 + t] = jnp.dot(hidden, wd_v[...], preferred_element_type=F32)
         send(part.at[40 + t], part.at[40 + t], small_send.at[2], small_recv.at[2], partner)
         wait_bytes(part.at[0], small_recv.at[2])
 
@@ -364,6 +445,8 @@
 
     def decode_rows():
         wait_bytes(ag.at[pl.ds(0, (N_CTX - 1) * PER)], small_recv.at[4])
+        for load in ups:
+            load.wait()
         to = lax.broadcasted_iota(jnp.int32, (QROWS, QROWS), 0)
         at = lax.broadcasted_iota(jnp.int32, (QROWS, QROWS), 1)
         source = lax.rem(to, 8) * 8 + lax.rem(to // 8, STEPS) * RPG + to // 16
@@ -375,7 +458,7 @@
         who = lax.rem(lax.broadcasted_iota(jnp.int32, (8, HD), 0), RPG)
         adapter = jnp.zeros((8, HD), jnp.int32)
         for b in range(RPG):
-            adapter = jnp.where(who == b, info[9 + b], adapter)
+            adapter = jnp.where(who == b, adapter_of[s * RPG + b], adapter)
         for kind in range(2):
             down = ag[40 + kind].astype(BF16).astype(F32)
             picked = jnp.where(lane == adapter, down, 0.0).astype(BF16)
@@ -383,6 +466,31 @@
                 n = 4 * kind + k
                 delta = jnp.dot(picked, up_v[n], preferred_element_type=F32)
                 tkv[n] = (ag[32 + n] + ADAPTER_SCALE * delta).astype(BF16).astype(F32)
+        which = lax.broadcasted_iota(jnp.int32, (QROWS, 8), 0)
+        other = lax.broadcasted_iota(jnp.int32, (QROWS, 8), 1)
+        tok_live = (
+            (lax.rem(other, RPG) == which // 16)
+            & (other // RPG <= lax.rem(which // 8, STEPS))
+            & (c == 0)
+        )
+        for k in range(HEADS):
+            tok = nt_dot(qp[k], tkv[k].astype(BF16)) * INV_ROOT
+            tok_max = jnp.max(jnp.where(tok_live, tok, NEG_FLOOR), axis=1, keepdims=True)
+            tok_w = jnp.where(tok_live, jnp.exp(tok - tok_max), 0.0)
+            tok_out = jnp.zeros((QROWS, HD), F32)
+            for i in range(8):
+                tok_out = tok_out + tok_w[:, i : i + 1] * tkv[4 + k, i : i + 1]
+            pst[0, k] = jnp.broadcast_to(tok_max, (QROWS, HD))
+            pst[1, k] = jnp.broadcast_to(jnp.sum(tok_w, axis=1, keepdims=True), (QROWS, HD))
+            pst[2, k] = tok_out
+
+    def merge(k, rows, block_max, total, out):
+        old = pst[0, k, rows]
+        top = jnp.maximum(old, block_max)
+        old_scale, scale = jnp.exp(old - top), jnp.exp(block_max - top)
+        pst[0, k, rows] = top
+        pst[1, k, rows] = old_scale * pst[1, k, rows] + scale * total
+        pst[2, k, rows] = old_scale * pst[2, k, rows] + scale * out
 
     def cache_block(b):
         @pl.when(b == 0)
@@ -390,7 +498,7 @@
             k_copy.wait()
             v_copy.wait()
 
-        left_len = info[b]
+        left_len = length_of[b] - c * CTX_DEV
         live = lax.broadcasted_iota(jnp.int32, (16, CTX_DEV), 1) < left_len
         rows = pl.ds(pl.multiple_of(b * 16, 16), 16)
         for k in range(HEADS):
@@ -399,100 +507,110 @@
             block_max = jnp.max(jnp.where(live, scores, NEG_FLOOR), axis=1, keepdims=True)
             weights = jnp.where(live, jnp.exp(scores - block_max), 0.0).astype(BF16)
             total = jnp.sum(weights.astype(F32), axis=1, keepdims=True)
-            pst[0, k, rows] = jnp.broadcast_to(block_max, (16, HD))
-            pst[1, k, rows] = jnp.broadcast_to(total, (16, HD))
-            pst[2, k, rows] = jnp.dot(weights, vc_v[b, :, cols], preferred_element_type=F32)
-
-    @pl.loop(0, UNITS + 6)
+            out = jnp.dot(weights, vc_v[b, :, cols], preferred_element_type=F32)
+            merge(k, rows, block_max, total, out)
+
+    stage1(0)
+    stage1(1)
+    down_rows()
+    page_rows()
+
+    @pl.loop(0, BLOCKS + 7)
     def _(i):
-        @pl.when(i < UNITS)
-        def _():
-            stage1(i)
-
-        @pl.when(i == 0)
-        def _():
+        @pl.when((i >= 1) & (i < UNITS - 1))
+        def _():
+            stage1(i + 1)
+
+        @pl.when((i >= 3) & (i < UNITS + 3))
+        def _():
+            stage4(i - 3)
+
+        @pl.when((i >= 2) & (i < UNITS + 2))
+        def _():
+            stage3(i - 2)
+
+        @pl.when((i >= 1) & (i < UNITS + 1))
+        def _():
+            stage2(i - 1)
+
+        @pl.when(i == 1)
+        def _():
+            across(0)
             decode_project()
 
-        @pl.when((i >= 3) & (i < UNITS + 3))
-        def _():
-            stage4(i - 3)
-
-        @pl.when((i >= 2) & (i < UNITS + 2))
-        def _():
-            stage3(i - 2)
-
-        @pl.when((i >= 1) & (i < UNITS + 1))
-        def _():
-            stage2(i - 1)
-
-        @pl.when(i == 1)
-        def _():
+        @pl.when(i == 2)
+        def _():
+            across(1)
             decode_sum()
             page_flags()
 
-        @pl.when(i == 2)
-        def _():
+        @pl.when(i == 3)
+        def _():
+            across(2)
+            across_again(0)
+            project_down()
             decode_rows()
 
-        @pl.when((i >= 3) & (i < 3 + RPG))
-        def _():
-            cache_block(i - 3)
-
-        @pl.when((i >= 4) & (i < UNITS + 4))
+        @pl.when(i == 4)
+        def _():
+            arrived(0, 3, 1)
+            across(3)
+
+        @pl.when(i == 5)
+        def _():
+            across_again(1)
+
+        @pl.when(i == 6)
+        def _():
+            across_again(2)
+
+        @pl.when(i == 7)
+        def _():
+            across_again(3)
+
+        @pl.when((i >= 4) & (i < 4 + RPG))
+        def _():
+            cache_block(i - 4)
+
+        @pl.when((i >= 4) & (i < BLOCKS + 4))
         def _():
             project(i - 4)
 
-        @pl.when((i >= 6) & (i < UNITS + 5))
-        def _():
-            place(i - 6)
+        @pl.when((i >= 6) & (i < BLOCKS + 6))
+        def _():
+            place(nth(i - 6, s_left))
 
         @pl.when(i >= 7)
         def _():
-            landed(i - 7)
-            write_out(i - 7)
+            landed(nth(i - 7, s_left))
+            write_out(nth(i - 7, s_left))
 
     landed(8)
 
+    page_request = target_of[s_left] - s * RPG
     live = nt_dot(jnp.ones((16, HD), BF16), pages[8]) > 0.5
-    which = lax.broadcasted_iota(jnp.int32, (QROWS, 8), 0)
-    other = lax.broadcasted_iota(jnp.int32, (QROWS, 8), 1)
-    tok_live = (
-        (lax.rem(other, RPG) == which // 16)
-        & (other // RPG <= lax.rem(which // 8, STEPS))
-        & (c == 0)
-    )
-    lane = lax.broadcasted_iota(jnp.int32, (16, HD), 1)
     for k in range(HEADS):
         query = jnp.zeros((16, HD), F32)
         for b in range(RPG):
-            query = jnp.where(info[4 + b] == 1, qp[k, b * 16 : b * 16 + 16].astype(F32), query)
+            query = jnp.where(page_request == b, qp[k, b * 16 : b * 16 + 16].astype(F32), query)
         scores = nt_dot(query.astype(BF16), pages[k]) * INV_ROOT
         p_max = jnp.max(jnp.where(live, scores, NEG_FLOOR), axis=1, keepdims=True)
         weights = jnp.where(live, jnp.exp(scores - p_max), 0.0).astype(BF16)
         p_total = jnp.sum(weights.astype(F32), axis=1, keepdims=True)
         p_out = jnp.dot(weights, pages[4 + k], preferred_element_type=F32)
-        tok = nt_dot(qp[k], tkv[k].astype(BF16)) * INV_ROOT
-        tok_max = jnp.max(jnp.where(tok_live, tok, NEG_FLOOR), axis=1, keepdims=True)
-        tok_w = jnp.where(tok_live, jnp.exp(tok - tok_max), 0.0)
-        tok_total = jnp.sum(tok_w, axis=1, keepdims=True)
-        tok_out = jnp.zeros((QROWS, HD), F32)
-        for i in range(8):
-            tok_out = tok_out + tok_w[:, i : i + 1] * tkv[4 + k, i : i + 1]
         for b in range(RPG):
             rows = slice(b * 16, b * 16 + 16)
-            wanted = info[4 + b] == 1
-            pm = jnp.where(wanted, p_max, NEG_FLOOR)
-            pt = jnp.where(wanted, p_total, 0.0)
-            po = jnp.where(wanted, p_out, 0.0)
-            cm = pst[0, k, rows]
-            tm = tok_max[rows]
-            top = jnp.maximum(jnp.maximum(cm, pm), tm)
-            c_scale, p_scale, t_scale = jnp.exp(cm - top), jnp.exp(pm - top), jnp.exp(tm - top)
-            total = c_scale * pst[1, k, rows] + p_scale * pt + t_scale * tok_total[rows]
-            mgs[k * 4 + b, 0] = (
-                c_scale * pst[2, k, rows] + p_scale * po + t_scale * tok_out[rows]
+            wanted = page_request == b
+            merge(
+                k,
+                rows,
+                jnp.where(wanted, p_max, NEG_FLOOR),
+                jnp.where(wanted, p_total, 0.0),
+                jnp.where(wanted, p_out, 0.0),
             )
-            mgs[k * 4 + b, 1] = jnp.where(lane < 64, top, total)
+            lane = lax.broadcasted_iota(jnp.int32, (16, HD), 1)
+            mgs[k * 4 + b, 0] = pst[2, k, rows]
+            mgs[k * 4 + b, 1] = jnp.where(lane < 64, pst[0, k, rows], pst[1, k, rows])
 
     @pl.loop(1, N_CTX)
     def _(j):
@@ -519,7 +637,14 @@
     @pl.loop(0, UNITS)
     def _(u):
         wait_bytes(w_v.at[u, pl.ds(0, 15 * SHARD)], g_send.at[u])
+
+    @pl.loop(0, BLOCKS + 1)
+    def _(u):
         wait_bytes(sendb.at[u, pl.ds(0, SLOT_ROWS - PAIR)], a_send.at[u])
+
+    for d, count in ((0, CUT), (1, SHARD - CUT)):
+        wait_bytes(w_v.at[0, pl.ds(0, 15 * SHARD)], x_send.at[d])
+        wait_bytes(w_v.at[0, pl.ds(0, 15 * count)], f_send.at[d])
 
     @pl.loop(0, 2 * HEADS)
     def _(n):
@@ -533,6 +658,27 @@
     wait_bytes(ag.at[pl.ds(0, (N_CTX - 1) * PER)], small_send.at[4])
     wait_bytes(mgr.at[pl.ds(0, N_CTX - 1)], small_send.at[5])
     wait_bytes(att.at[pl.ds(0, N_CTX - 1)], small_send.at[6])
+    wait_bytes(dt_v.at[:, pl.ds(0, (N_CTX - 1) * SHARD)], small_send.at[7])
+
+
+def finish_kernel(pk, pv, att, pk_out, pv_out, att_out, rows, sem):
+    copies = [
+        pltpu.make_async_copy(pk, pk_out, sem.at[0]),
+        pltpu.make_async_copy(pv, pv_out, sem.at[1]),
+    ]
+    for copy in copies:
+        copy.start()
+    for k in range(HEADS):
+        for b in range(RPG):
+            block = att[k * RPG + b].astype(F32)
+            for step in range(STEPS):
+                for g in range(8):
+                    cols = slice((k * 8 + g) * HD, (k * 8 + g + 1) * HD)
+                    at = step * 8 + g
+                    rows[step, b : b + 1, cols] = block[at : at + 1]
+    att_out[...] = rows[...].astype(BF16)
+    for copy in copies:
+        copy.wait()
 
 
 def on_device(
@@ -551,35 +697,6 @@
     request_context_length,
     page_owner_index,
 ):
-    n_section = lax.axis_size("section")
-    section_at = lax.axis_index("section")
-    ctx_at = lax.axis_index("ctx")
-    span_request = pick_entry(prefill_request_target, section_at)
-    span_adapter = pick_entry(request_adapter_index, span_request)
-    page_request = pick_entry(prefill_request_target, (section_at + n_section - 1) % n_section)
-    local_ids = section_at * RPG + jnp.arange(RPG, dtype=jnp.int32)
-    batch_ids = jnp.arange(request_adapter_index.shape[0], dtype=jnp.int32)
-    adapters = jnp.sum(
-        jnp.where(local_ids[:, None] == batch_ids[None, :], request_adapter_index[None, :], 0),
-        axis=1,
-    )
-    info = jnp.concatenate(
-        [
-            request_context_length - ctx_at * CTX_DEV,
-            (local_ids == page_request).astype(jnp.int32),
-            span_adapter[None],
-            adapters,
-            jnp.zeros((3,), jnp.int32),
-        ]
-    ).astype(jnp.int32)
-    owners = page_owner_index[:, 0]
-    order = jnp.arange(owners.shape[0], dtype=jnp.int32)
-    earlier = (owners[None, :] == owners[:, None]) & (order[None, :] < order[:, None])
-    slot_of = owners * 2 + jnp.sum(earlier, axis=1).astype(jnp.int32)
-    drow = (slot_of[:, None] * BLK + jnp.arange(BLK, dtype=jnp.int32)[None, :]).reshape(1, ROWS)
-    drow = jnp.broadcast_to(drow, (8, ROWS))
-    decode_rows = decode_hidden_states.reshape(STEPS * RPG, SHARD)
-
     hbm = pl.BlockSpec(memory_space=pl.ANY)
     vmem = pl.BlockSpec(memory_space=pltpu.VMEM)
     smem = pl.BlockSpec(memory_space=pltpu.SMEM)
@@ -591,12 +708,15 @@
             jax.ShapeDtypeStruct((SLOT_ROWS, HEADS * HD), BF16),
             jax.ShapeDtypeStruct((N_CTX, 16, HD), BF16),
         ),
-        in_specs=[smem, vmem, vmem] + [hbm] * 9,
+        in_specs=[smem] * 4 + [vmem] + [hbm] * 9,
         out_specs=(hbm, hbm, vmem),
         scratch_shapes=[
             pltpu.VMEM((ROWS, 8192), BF16),
-            pltpu.VMEM((UNITS, 8192, HD), BF16),
+            pltpu.VMEM((BLOCKS, 8192, HD), BF16),
             pltpu.VMEM((SHARD, 4096), BF16),
+            pltpu.VMEM((SHARD, HD), BF16),
+            pltpu.VMEM((ADAPTER_RANK, 8192), BF16),
+            pltpu.VMEM((8, SHARD), F32),
             pltpu.VMEM((8, HD, HD), BF16),
             pltpu.VMEM((RPG, CTX_DEV, HEADS * HD), BF16),
             pltpu.VMEM((RPG, CTX_DEV, HEADS * HD), BF16),
@@ -605,6 +725,7 @@
             pltpu.VMEM((8, ROWS, HD), BF16),
             pltpu.VMEM((8, ROWS, HD), BF16),
             pltpu.VMEM((SLOT_ROWS, ROWS), BF16),
+            pltpu.VMEM((8, ROWS), jnp.int32),
             pltpu.VMEM((8, ROWS), jnp.int32),
             pltpu.VMEM((9, SLOT_ROWS, HD), BF16),
             pltpu.VMEM((9, SLOT_ROWS, HD), BF16),
@@ -617,19 +738,23 @@
             pltpu.VMEM((N_CTX, 2, 16, HD), F32),
             pltpu.VMEM((N_CTX, 2, 16, HD), F32),
             pltpu.VMEM((N_CTX, 16, HD), BF16),
-            dma((UNITS,)),
+            dma((9,)),
             dma,
             dma,
             dma((2,)),
             dma((8,)),
             dma((UNITS, 4)),
             dma((UNITS,)),
+            dma((2, 4)),
+            dma((2,)),
+            dma((2,)),
+            dma((2,)),
             dma((8,)),
             dma((8,)),
             dma((9,)),
             dma((9,)),
-            dma((7,)),
-            dma((7,)),
+            dma((8,)),
+            dma((8,)),
             dma((8,)),
         ],
         compiler_params=pltpu.CompilerParams(
@@ -639,9 +764,11 @@
             flops=12_000_000_000, bytes_accessed=30_000_000, transcendentals=600_000
         ),
     )(
-        info,
-        decode_rows,
-        drow,
+        request_adapter_index,
+        prefill_request_target,
+        request_context_length,
+        page_owner_index,
+        decode_hidden_states,
         prefill_hidden_states,
         query_matrix,
         key_matrix,
@@ -653,8 +780,18 @@
         request_value_cache,
     )
     page_shape = (SLOT_ROWS // BLK, BLK, HEADS * HD)
-    attended = attended.reshape(HEADS, RPG, STEPS, H // KVH, HD)
-    attended = jnp.transpose(attended, (2, 1, 0, 3, 4)).reshape(STEPS, RPG, HEADS * 8 * HD)
+    page_keys, page_values, attended = pl.pallas_call(
+        finish_kernel,
+        out_shape=(
+            jax.ShapeDtypeStruct((SLOT_ROWS, HEADS * HD), BF16),
+            jax.ShapeDtypeStruct((SLOT_ROWS, HEADS * HD), BF16),
+            jax.ShapeDtypeStruct((STEPS, RPG, HEADS * 8 * HD), BF16),
+        ),
+        in_specs=[hbm, hbm, vmem],
+        out_specs=(hbm, hbm, vmem),
+        scratch_shapes=[pltpu.VMEM((STEPS, RPG, HEADS * 8 * HD), F32), dma((2,))],
+        compiler_params=pltpu.CompilerParams(vmem_limit_bytes=4 * 1024 * 1024),
+    )(page_keys, page_values, attended)
     return (page_keys.reshape(page_shape), page_values.reshape(page_shape), attended)
 
 

time: 176 us -> 141 us (0.80)
  Pallas kernels: 159 us -> 136 us
  other arithmetic: 7.03 us -> 0 us
  local copies, waits for them, and re-layouts: 9.4 us -> 4.61 us
    pallas_call x1, Pallas kernels: 159 us -> 134 us  [on_device(): pl.pallas_call(layer_kernel, out_shape=(jax.ShapeDtypeStruct((SLOT_ROWS,...]
    reduce_sum x4 -> x0, other arithmetic: 4.98 us -> none  [the longest x2 3.23 us: pick_entry(): return jnp.sum(jnp.where(places == wanted, table, 0))]
    pallas_call x0 -> x1, Pallas kernels: none -> 1.96 us  [on_device(): pl.pallas_call(finish_kernel, out_shape=(jax.ShapeDtypeStruct((SLOT_ROWS,...]
    reshape x2 -> x0, local copies, waits for them, and re-layouts: 1.96 us -> none  [the longest x1 1.31 us: on_device(): decode_rows = decode_hidden_states.reshape(STEPS * RPG, SHARD)]
    unnamed x2 -> x7, local copies, waits for them, and re-layouts: 4.61 us -> 4.61 us
where the time goes in v2:
time: 141 us
  Pallas kernels  136 us (96%)
  local copies, waits for them, and re-layouts  4.61 us (3%)
    pallas_call x1, Pallas kernels, on_device(): pl.pallas_call(layer_kernel, out_shape=(jax.ShapeDtypeStruct((SLOT_ROWS,...  134 us
    unnamed x7, local copies, waits for them, and re-layouts  4.61 us

profile of v2, /device:TPU:0, one launch (start us, length us, event | category | flops | bytes accessed | tf_op | source)
XLA Modules:
  0.0 141.2 jit_solution(5206746053928045988)
XLA Ops:
  0.6 1.3 copy.17.owner_of
  2.0 134.0 %shard_map.157 = (bf16[1024,512]{1,0:T(8,128)(2,1)}, bf16[1024,512]{1,0:T(8,128)(2,1)}, bf16[16,16,128]{2,1,0:T(8,128)(2,1)}) custom-call(s32[16]{0:T(128)} %adapter_of.1, s32[4]{0:T(128)} %target_of.1, s32[4]{0:T(128)} %length_of.1, s32[16,1]{1,0:T(8,128)} %copy.17.owner_of, bf16[2,4,512]{2,1,0:T(4,128)(2,1)} %xd.1, bf16[512,8192]{1,0:T(8,128)(2,1)} %x_hbm.1, ...), custom_call_target="tpu_custom_call" | custom-call | flops 12000000000 | bytes 30000000 | tf_op jit(solution)/shard_map/pallas_call | solution.py:704
  136.0 0.0 copy-start
  136.0 1.2 copy-done
  137.2 0.0 copy-start.1
  137.2 1.2 copy-done.1
  138.4 0.0 copy-start.2
  138.4 0.8 copy-done.2
  139.2 2.0 %shard_map.158 = (bf16[1024,512]{1,0:T(8,128)(2,1)}, bf16[1024,512]{1,0:T(8,128)(2,1)}, bf16[2,4,4096]{2,1,0:T(4,128)(2,1)}) custom-call(bf16[1024,512]{1,0:T(8,128)(2,1)S(1)} %copy-done, bf16[1024,512]{1,0:T(8,128)(2,1)S(1)} %copy-done.1, bf16[16,16,128]{2,1,0:T(8,128)(2,1)S(1)} %copy-done.2), custom_call_target="tpu_custom_call" | custom-call | tf_op jit(solution)/shard_map/pallas_call | solution.py:783
Async XLA Ops:
  136.0 1.2 copy-start
  137.2 1.2 copy-start.1
  138.4 0.8 copy-start.2

commit v3 on v2

--- a/solution.py
+++ b/solution.py
@@ -23,6 +23,8 @@
 N_CTX = 16
 SHARD = 512
 UNITS = 5
+HALVES = 2 * UNITS
+HALF = 256
 BLOCKS = 8
 HEADS = 4
 ROWS = 512
@@ -34,6 +36,15 @@
 DBLOCKS = 48
 PER = 3
 
+PROJECT_AT = (9, 11, 12, 13, 14, 15, 17, 18)
+PLACE_AT = tuple(at + 2 for at in PROJECT_AT)
+LAND_AT = tuple(at + 4 for at in PROJECT_AT)
+CACHE_AT = (10, 14, 16, 18)
+ADD_LAG = (3, 5, 7, 8)
+ACROSS_AT = (9, 11, 12, 12)
+FAR_AT = (15, 17, 18, 18)
+LAST = LAND_AT[-1]
+
 MESH = pl.DeviceIdType.MESH
 F32 = jnp.float32
 BF16 = jnp.bfloat16
@@ -41,6 +52,14 @@
 
 def wait_bytes(ref, sem):
     pltpu.make_async_copy(ref, ref, sem).wait()
+
+
+def turn(i, slots):
+    here, which = False, -1
+    for at in slots:
+        here = here | (i == at)
+        which = which + jnp.where(i >= at, 1, 0)
+    return here, which
 
 
 def nt_dot(a, b):
@@ -75,6 +94,7 @@
     kc_v,
     vc_v,
     acc,
+    accs,
     dn,
     row,
     raw,
@@ -89,6 +109,8 @@
     qp,
     tkv,
     pst,
+    pgw,
+    pgs,
     mgs,
     mgr,
     att,
@@ -184,31 +206,32 @@
     for load in shard_loads:
         load.wait()
 
-    def pass_on(u, stage, shard, first, count, ctx):
-        rows = pl.ds(pl.multiple_of(shard * SHARD + first, 128), count)
-        piece = w_v.at[block_of(u), rows]
-        send(piece, piece, g_send.at[u], g_recv.at[u, stage], here(ctx))
-
-    def block_of(u):
+    def block_of(h):
+        u = h // 2
         return jnp.where(u == 0, HEADS + s, u - 1)
 
-    def arrived(u, stage, shards):
-        wait_bytes(w_v.at[block_of(u), pl.ds(0, shards * SHARD)], g_recv.at[u, stage])
+    def pass_on(h, stage, shard, first, count, ctx):
+        start = shard * SHARD + lax.rem(h, 2) * HALF + first
+        piece = w_v.at[block_of(h), pl.ds(pl.multiple_of(start, 64), count)]
+        send(piece, piece, g_send.at[h], g_recv.at[h, stage], here(ctx))
+
+    def arrived(h, stage, shards):
+        wait_bytes(w_v.at[block_of(h), pl.ds(0, shards * HALF)], g_recv.at[h, stage])
 
     yp, ym, zp, zm = chip(1, 0), chip(-1, 0), chip(0, 1), chip(0, -1)
     A, B, A0, A1, B0, B1, ZERO = (
-        (0, 256),
-        (256, 256),
+        (0, 128),
         (128, 128),
-        (0, 128),
-        (256, 128),
-        (384, 128),
-        (128, 256),
+        (64, 64),
+        (0, 64),
+        (128, 64),
+        (192, 64),
+        (64, 128),
     )
 
     def stage1(u):
         for ctx in (yp, zp, ym, zm):
-            pass_on(u, 0, c, 0, SHARD, ctx)
+            pass_on(u, 0, c, 0, HALF, ctx)
 
     def stage2(u):
         arrived(u, 0, 4)
@@ -252,9 +275,9 @@
         (chip(2, 2),),
     )
 
-    def across(group):
+    def across(group, half):
         for shard in GROUPS[group]:
-            rows = pl.ds(pl.multiple_of(shard * SHARD, SHARD), SHARD)
+            rows = pl.ds(pl.multiple_of(shard * SHARD + half * HALF, HALF), HALF)
             piece = w_v.at[HEADS + s, rows]
             send(piece, piece, x_send.at[0], x_recv.at[0, group], right)
             send(piece, piece, x_send.at[1], x_recv.at[1, group], left)
@@ -266,10 +289,10 @@
         for shard in GROUPS[group]:
             rows = pl.ds(pl.multiple_of(shard * SHARD, SHARD), CUT)
             piece = w_v.at[HEADS + s_left, rows]
-            send(piece, piece, f_send.at[0], f_recv.at[0], right)
+            send(piece, piece, f_send.at[0], f_recv.at[0, group], right)
             rows = pl.ds(pl.multiple_of(shard * SHARD + CUT, 128), SHARD - CUT)
             piece = w_v.at[HEADS + s_right, rows]
-            send(piece, piece, f_send.at[1], f_recv.at[1], left)
+            send(piece, piece, f_send.at[1], f_recv.at[1, group], left)
 
     span_request = target_of[s]
     span_adapter = jnp.int32(0)
@@ -291,7 +314,8 @@
             send(piece, piece, small_send.at[7], small_recv.at[7], here(ctx))
 
     def project_down():
-        x_copy.wait()
+        for load in ups:
+            load.wait()
         wait_bytes(dt_v.at[:, pl.ds(0, (N_CTX - 1) * SHARD)], small_recv.at[7])
         acc[...] = jnp.zeros_like(acc)
 
@@ -304,35 +328,45 @@
         dn[t] = jnp.dot(down, pick, preferred_element_type=F32).astype(BF16)
         send(dn.at[t], dn.at[t], small_send.at[1], small_recv.at[1], partner)
 
+    def add_shards(n, shards, first, count):
+        parts = [
+            pl.ds(pl.multiple_of(shard * SHARD + first, HALF), count) for shard in shards
+        ]
+
+        @pl.loop(0, 2)
+        def _(m):
+            some = pl.ds(pl.multiple_of(m * 256, 256), 256)
+            hidden = jnp.concatenate([x_v[some, part] for part in parts], axis=1)
+            weight = jnp.concatenate([w_v[n, part] for part in parts], axis=0)
+            accs[n, some] += jnp.dot(hidden, weight, preferred_element_type=F32)
+
+    def add_across(group):
+        shards = GROUPS[group] + ((c,) if group == 0 else ())
+        add_shards(HEADS + s_left, shards, 0, SHARD)
+        add_shards(HEADS + s_right, shards, 0, SHARD)
+
+    def add_far(group):
+        count = len(GROUPS[group])
+        n = HEADS + s_far
+        wait_bytes(w_v.at[n, pl.ds(0, count * CUT)], f_recv.at[0, group])
+        wait_bytes(w_v.at[n, pl.ds(0, count * (SHARD - CUT))], f_recv.at[1, group])
+        add_shards(n, GROUPS[group] + ((c,) if group == 0 else ()), 0, SHARD)
+
     def nth(p, sec):
-        far = jnp.where(p == 5, sec + n_sec - 1, jnp.where(p == 6, sec + 1, sec + 2))
-        value = HEADS + jnp.where(p == 0, sec, lax.rem(far, n_sec))
-        return jnp.where((p >= 1) & (p <= HEADS), p - 1, value)
+        keys = jnp.where(p == 6, 3, p // 2)
+        ahead = jnp.where(p == 2, n_sec - 1, jnp.where(p == 4, 1, jnp.where(p == 7, 2, 0)))
+        is_key = (p == 1) | (p == 3) | (p == 5) | (p == 6)
+        return jnp.where(is_key, keys, HEADS + lax.rem(sec + ahead, n_sec))
 
     def project(p):
         n = nth(p, s)
 
-        @pl.when((p >= 1) & (p < UNITS))
-        def _():
-            arrived(p, 3, 1)
-
         @pl.when(p == 0)
         def _():
             wait_bytes(dn.at[0], small_recv.at[1])
 
-        @pl.when(p == BLOCKS - 1)
-        def _():
-            wait_bytes(w_v.at[n, pl.ds(0, 15 * CUT)], f_recv.at[0])
-            wait_bytes(w_v.at[n, pl.ds(0, 15 * (SHARD - CUT))], f_recv.at[1])
-
-        acc[...] = jnp.dot(dn[n // HEADS], up_v[n], preferred_element_type=F32) * ADAPTER_SCALE
-
-        @pl.loop(0, 8)
-        def _(i):
-            part_k = pl.ds(pl.multiple_of(i * 1024, 1024), 1024)
-            acc[...] += jnp.dot(x_v[:, part_k], w_v[n, part_k], preferred_element_type=F32)
-
-        row[n] = acc[...].astype(BF16)
+        delta = jnp.dot(dn[n // HEADS], up_v[n], preferred_element_type=F32)
+        row[n] = (accs[n] + ADAPTER_SCALE * delta).astype(BF16)
         send(row.at[n], raw.at[n], row_send.at[n], row_recv.at[n], right)
 
     def exchange(n):
@@ -361,15 +395,20 @@
         exchange(n)
 
     def page_rows():
-        owners = [owner_of[i, 0] for i in range(16)]
-        lane = lax.broadcasted_iota(jnp.int32, (8, ROWS), 1)
-        rows = jnp.zeros((8, ROWS), jnp.int32)
-        for i in range(16):
-            slot = owners[i] * 2
-            for j in range(i):
-                slot = slot + jnp.where(owners[j] == owners[i], 1, 0)
-            rows = jnp.where(lane // BLK == i, slot * BLK + lax.rem(lane, BLK), rows)
-        drow[...] = rows
+        first = lax.broadcasted_iota(jnp.int32, (16, 16), 0)
+        second = lax.broadcasted_iota(jnp.int32, (16, 16), 1)
+        across_ids = jnp.broadcast_to(owner_of[...].astype(F32), (16, 16))
+        ids = jnp.sum(jnp.where(first == second, across_ids, 0.0), axis=1, keepdims=True)
+        before = (ids == across_ids) & (second < first)
+        rank = jnp.sum(jnp.where(before, 1.0, 0.0), axis=1, keepdims=True)
+        slot_row = (ids * 2 + rank) * BLK
+        page = lax.broadcasted_iota(jnp.int32, (16, ROWS), 0)
+        lane = lax.broadcasted_iota(jnp.int32, (16, ROWS), 1)
+        token = lax.rem(lane, BLK).astype(F32)
+        rows = jnp.sum(
+            jnp.where(lane // BLK == page, slot_row + token, 0.0), axis=0, keepdims=True
+        )
+        drow[...] = jnp.broadcast_to(rows, (8, ROWS)).astype(jnp.int32)
         send(drow, drow_r, small_send.at[0], small_recv.at[0], right)
 
     def page_flags():
@@ -418,6 +457,8 @@
             blocks(jnp.dot(hidden, w_v[n, mine], preferred_element_type=F32), 32 + n)
         part[40 + t] = jnp.dot(hidden, wd_v[...], preferred_element_type=F32)
         send(part.at[40 + t], part.at[40 + t], small_send.at[2], small_recv.at[2], partner)
+
+    def decode_spread():
         wait_bytes(part.at[0], small_recv.at[2])
 
         @pl.loop(1, N_CTX)
@@ -445,8 +486,6 @@
 
     def decode_rows():
         wait_bytes(ag.at[pl.ds(0, (N_CTX - 1) * PER)], small_recv.at[4])
-        for load in ups:
-            load.wait()
         to = lax.broadcasted_iota(jnp.int32, (QROWS, QROWS), 0)
         at = lax.broadcasted_iota(jnp.int32, (QROWS, QROWS), 1)
         source = lax.rem(to, 8) * 8 + lax.rem(to // 8, STEPS) * RPG + to // 16
@@ -510,86 +549,10 @@
             out = jnp.dot(weights, vc_v[b, :, cols], preferred_element_type=F32)
             merge(k, rows, block_max, total, out)
 
-    stage1(0)
-    stage1(1)
-    down_rows()
-    page_rows()
-
-    @pl.loop(0, BLOCKS + 7)
-    def _(i):
-        @pl.when((i >= 1) & (i < UNITS - 1))
-        def _():
-            stage1(i + 1)
-
-        @pl.when((i >= 3) & (i < UNITS + 3))
-        def _():
-            stage4(i - 3)
-
-        @pl.when((i >= 2) & (i < UNITS + 2))
-        def _():
-            stage3(i - 2)
-
-        @pl.when((i >= 1) & (i < UNITS + 1))
-        def _():
-            stage2(i - 1)
-
-        @pl.when(i == 1)
-        def _():
-            across(0)
-            decode_project()
-
-        @pl.when(i == 2)
-        def _():
-            across(1)
-            decode_sum()
-            page_flags()
-
-        @pl.when(i == 3)
-        def _():
-            across(2)
-            across_again(0)
-            project_down()
-            decode_rows()
-
-        @pl.when(i == 4)
-        def _():
-            arrived(0, 3, 1)
-            across(3)
-
-        @pl.when(i == 5)
-        def _():
-            across_again(1)
-
-        @pl.when(i == 6)
-        def _():
-            across_again(2)
-
-        @pl.when(i == 7)
-        def _():
-            across_again(3)
-
-        @pl.when((i >= 4) & (i < 4 + RPG))
-        def _():
-            cache_block(i - 4)
-
-        @pl.when((i >= 4) & (i < BLOCKS + 4))
-        def _():
-            project(i - 4)
-
-        @pl.when((i >= 6) & (i < BLOCKS + 6))
-        def _():
-            place(nth(i - 6, s_left))
-
-        @pl.when(i >= 7)
-        def _():
-            landed(nth(i - 7, s_left))
-            write_out(nth(i - 7, s_left))
-
-    landed(8)
-
     page_request = target_of[s_left] - s * RPG
-    live = nt_dot(jnp.ones((16, HD), BF16), pages[8]) > 0.5
-    for k in range(HEADS):
+
+    def page_scores(k):
+        live = nt_dot(jnp.ones((16, HD), BF16), pages[8]) > 0.5
         query = jnp.zeros((16, HD), F32)
         for b in range(RPG):
             query = jnp.where(page_request == b, qp[k, b * 16 : b * 16 + 16].astype(F32), query)
@@ -597,25 +560,159 @@
         p_max = jnp.max(jnp.where(live, scores, NEG_FLOOR), axis=1, keepdims=True)
         weights = jnp.where(live, jnp.exp(scores - p_max), 0.0).astype(BF16)
         p_total = jnp.sum(weights.astype(F32), axis=1, keepdims=True)
-        p_out = jnp.dot(weights, pages[4 + k], preferred_element_type=F32)
+        pgw[k] = weights
+        pgs[0, k] = jnp.broadcast_to(p_max, (16, HD))
+        pgs[1, k] = jnp.broadcast_to(p_total, (16, HD))
+
+    def page_merge(k):
+        p_out = jnp.dot(pgw[k], pages[HEADS + k], preferred_element_type=F32)
+        lane = lax.broadcasted_iota(jnp.int32, (16, HD), 1)
         for b in range(RPG):
             rows = slice(b * 16, b * 16 + 16)
             wanted = page_request == b
             merge(
                 k,
                 rows,
-                jnp.where(wanted, p_max, NEG_FLOOR),
-                jnp.where(wanted, p_total, 0.0),
+                jnp.where(wanted, pgs[0, k], NEG_FLOOR),
+                jnp.where(wanted, pgs[1, k], 0.0),
                 jnp.where(wanted, p_out, 0.0),
             )
-            lane = lax.broadcasted_iota(jnp.int32, (16, HD), 1)
-            mgs[k * 4 + b, 0] = pst[2, k, rows]
-            mgs[k * 4 + b, 1] = jnp.where(lane < 64, pst[0, k, rows], pst[1, k, rows])
-
-    @pl.loop(1, N_CTX)
-    def _(j):
-        ctx = lax.rem(c + j, N_CTX)
-        send(mgs.at[ctx], mgr.at[c], small_send.at[5], small_recv.at[5], here(ctx))
+            mgs[k * RPG + b, 0] = pst[2, k, rows]
+            mgs[k * RPG + b, 1] = jnp.where(lane < 64, pst[0, k, rows], pst[1, k, rows])
+            ctx = k * RPG + b
+
+            @pl.when(ctx != c)
+            def _():
+                send(mgs.at[ctx], mgr.at[c], small_send.at[5], small_recv.at[5], here(ctx))
+
+    stage1(0)
+    stage1(1)
+    down_rows()
+    page_rows()
+    accs[...] = jnp.zeros_like(accs)
+
+    @pl.loop(2, LAST)
+    def _(i):
+        @pl.when((i >= 6) & (i < HALVES + 6))
+        def _():
+            stage4(i - 6)
+
+        @pl.when((i >= 4) & (i < HALVES + 4))
+        def _():
+            stage3(i - 4)
+
+        @pl.when((i >= 2) & (i < HALVES + 2))
+        def _():
+            stage2(i - 2)
+
+        @pl.when(i < HALVES)
+        def _():
+            stage1(i)
+
+        @pl.when((i >= 8) & (i < HALVES + 8))
+        def _():
+            arrived(i - 8, 3, 1)
+
+        for group in range(4):
+
+            @pl.when((i == 2 + 2 * group) | (i == 3 + 2 * group))
+            def _(group=group):
+                across(group, lax.rem(i, 2))
+
+        for group, at in enumerate(ACROSS_AT):
+
+            @pl.when(i == at)
+            def _(group=group):
+                across_again(group)
+
+        @pl.when(i == ADD_LAG[0])
+        def _():
+            x_copy.wait()
+
+        for stage, lag in enumerate(ADD_LAG):
+
+            @pl.when((i >= lag) & (i < HALVES + lag))
+            def _(stage=stage, lag=lag):
+                shards = GROUPS[stage] + ((c,) if stage == 0 else ())
+                h = i - lag
+                add_shards(block_of(h), shards, lax.rem(h, 2) * HALF, HALF)
+
+        for group, at in enumerate(ACROSS_AT):
+
+            @pl.when(i == at)
+            def _(group=group):
+                add_across(group)
+
+        for group, at in enumerate(FAR_AT):
+
+            @pl.when(i == at)
+            def _(group=group):
+                add_far(group)
+
+        @pl.when(i == 4)
+        def _():
+            decode_project()
+
+        @pl.when(i == 5)
+        def _():
+            decode_spread()
+
+        @pl.when(i == 6)
+        def _():
+            page_flags()
+
+        @pl.when(i == 7)
+        def _():
+            decode_sum()
+
+        @pl.when(i == 8)
+        def _():
+            project_down()
+
+        now, p = turn(i, PROJECT_AT)
+
+        @pl.when(now)
+        def _():
+            project(p)
+
+        @pl.when(i == 9)
+        def _():
+            decode_rows()
+
+        now, q = turn(i, PLACE_AT)
+
+        @pl.when(now)
+        def _():
+            place(nth(q, s_left))
+
+        now, b = turn(i, CACHE_AT)
+
+        @pl.when(now)
+        def _():
+            cache_block(b)
+
+        @pl.when(i == LAND_AT[0])
+        def _():
+            landed(8)
+
+        now, r = turn(i, LAND_AT)
+
+        @pl.when(now)
+        def _():
+            n = nth(r, s_left)
+            landed(n)
+            write_out(n)
+
+            @pl.when(n < HEADS)
+            def _():
+                page_scores(n)
+
+    for r in (0, 2, 4):
+        page_merge(nth(r, s_left) - HEADS)
+    far = nth(BLOCKS - 1, s_left)
+    landed(far)
+    page_merge(far - HEADS)
+    write_out(far)
 
     mgr[c] = mgs[c]
     wait_bytes(mgr.at[pl.ds(0, N_CTX - 1)], small_recv.at[5])
@@ -634,9 +731,9 @@
     wait_bytes(att.at[pl.ds(0, N_CTX - 1)], small_recv.at[6])
     att_out[...] = att[...]
 
-    @pl.loop(0, UNITS)
-    def _(u):
-        wait_bytes(w_v.at[u, pl.ds(0, 15 * SHARD)], g_send.at[u])
+    @pl.loop(0, HALVES)
+    def _(h):
+        wait_bytes(w_v.at[0, pl.ds(0, 15 * HALF)], g_send.at[h])
 
     @pl.loop(0, BLOCKS + 1)
     def _(u):
@@ -661,13 +758,20 @@
     wait_bytes(dt_v.at[:, pl.ds(0, (N_CTX - 1) * SHARD)], small_send.at[7])
 
 
-def finish_kernel(pk, pv, att, pk_out, pv_out, att_out, rows, sem):
-    copies = [
-        pltpu.make_async_copy(pk, pk_out, sem.at[0]),
-        pltpu.make_async_copy(pv, pv_out, sem.at[1]),
-    ]
-    for copy in copies:
-        copy.start()
+def finish_kernel(pk, pv, att, pk_out, pv_out, att_out, held, rows, in_sem, out_sem):
+    parts = [(j, i) for i in range(4) for j in range(2)]
+
+    def moves(j, i):
+        some = pl.ds(i * (SLOT_ROWS // 4), SLOT_ROWS // 4)
+        source, result = (pk, pv)[j], (pk_out, pv_out)[j]
+        return (
+            pltpu.make_async_copy(source.at[some], held.at[j, some], in_sem.at[j, i]),
+            pltpu.make_async_copy(held.at[j, some], result.at[some], out_sem.at[j, i]),
+        )
+
+    copies = [moves(j, i) for j, i in parts]
+    for into, _ in copies:
+        into.start()
     for k in range(HEADS):
         for b in range(RPG):
             block = att[k * RPG + b].astype(F32)
@@ -677,8 +781,11 @@
                     at = step * 8 + g
                     rows[step, b : b + 1, cols] = block[at : at + 1]
     att_out[...] = rows[...].astype(BF16)
-    for copy in copies:
-        copy.wait()
+    for into, out in copies:
+        into.wait()
+        out.start()
+    for _, out in copies:
+        out.wait()
 
 
 def on_device(
@@ -708,7 +815,7 @@
             jax.ShapeDtypeStruct((SLOT_ROWS, HEADS * HD), BF16),
             jax.ShapeDtypeStruct((N_CTX, 16, HD), BF16),
         ),
-        in_specs=[smem] * 4 + [vmem] + [hbm] * 9,
+        in_specs=[smem] * 3 + [vmem] * 2 + [hbm] * 9,
         out_specs=(hbm, hbm, vmem),
         scratch_shapes=[
             pltpu.VMEM((ROWS, 8192), BF16),
@@ -721,6 +828,7 @@
             pltpu.VMEM((RPG, CTX_DEV, HEADS * HD), BF16),
             pltpu.VMEM((RPG, CTX_DEV, HEADS * HD), BF16),
             pltpu.VMEM((ROWS, HD), F32),
+            pltpu.VMEM((BLOCKS, ROWS, HD), F32),
             pltpu.VMEM((2, ROWS, HD), BF16),
             pltpu.VMEM((8, ROWS, HD), BF16),
             pltpu.VMEM((8, ROWS, HD), BF16),
@@ -735,6 +843,8 @@
             pltpu.VMEM((HEADS, QROWS, HD), BF16),
             pltpu.VMEM((8, 8, HD), F32),
             pltpu.VMEM((3, HEADS, QROWS, HD), F32),
+            pltpu.VMEM((HEADS, 16, SLOT_ROWS), BF16),
+            pltpu.VMEM((2, HEADS, 16, HD), F32),
             pltpu.VMEM((N_CTX, 2, 16, HD), F32),
             pltpu.VMEM((N_CTX, 2, 16, HD), F32),
             pltpu.VMEM((N_CTX, 16, HD), BF16),
@@ -743,11 +853,11 @@
             dma,
             dma((2,)),
             dma((8,)),
-            dma((UNITS, 4)),
-            dma((UNITS,)),
+            dma((HALVES, 4)),
+            dma((HALVES,)),
             dma((2, 4)),
             dma((2,)),
-            dma((2,)),
+            dma((2, 4)),
             dma((2,)),
             dma((8,)),
             dma((8,)),
@@ -767,7 +877,7 @@
         request_adapter_index,
         prefill_request_target,
         request_context_length,
-        page_owner_index,
+        page_owner_index.reshape(1, 16),
         decode_hidden_states,
         prefill_hidden_states,
         query_matrix,
@@ -789,8 +899,13 @@
         ),
         in_specs=[hbm, hbm, vmem],
         out_specs=(hbm, hbm, vmem),
-        scratch_shapes=[pltpu.VMEM((STEPS, RPG, HEADS * 8 * HD), F32), dma((2,))],
-        compiler_params=pltpu.CompilerParams(vmem_limit_bytes=4 * 1024 * 1024),
+        scratch_shapes=[
+            pltpu.VMEM((2, SLOT_ROWS, HEADS * HD), BF16),
+            pltpu.VMEM((STEPS, RPG, HEADS * 8 * HD), F32),
+            dma((2, 4)),
+            dma((2, 4)),
+        ],
+        compiler_params=pltpu.CompilerParams(vmem_limit_bytes=58 * 1024 * 1024),
     )(page_keys, page_values, attended)
     return (page_keys.reshape(page_shape), page_values.reshape(page_shape), attended)
 

time: 141 us -> 124 us (0.88)
  Pallas kernels: 136 us -> 123 us
  local copies, waits for them, and re-layouts: 4.61 us -> 0 us
    pallas_call x1, Pallas kernels: 134 us -> 120 us  [on_device(): pl.pallas_call(layer_kernel, out_shape=(jax.ShapeDtypeStruct((SLOT_ROWS,...]
    unnamed x7 -> x0, local copies, waits for them, and re-layouts: 4.61 us -> none
    pallas_call x1, Pallas kernels: 1.96 us -> 3.86 us  [on_device(): pl.pallas_call(finish_kernel, out_shape=(jax.ShapeDtypeStruct((SLOT_ROWS,...]
where the time goes in v3:
time: 124 us
  Pallas kernels  123 us (99%)
    pallas_call x1, Pallas kernels, on_device(): pl.pallas_call(layer_kernel, out_shape=(jax.ShapeDtypeStruct((SLOT_ROWS,...  120 us
    pallas_call x1, Pallas kernels, on_device(): pl.pallas_call(finish_kernel, out_shape=(jax.ShapeDtypeStruct((SLOT_ROWS,...  3.86 us

profile of v3, /device:TPU:0, one launch (start us, length us, event | category | flops | bytes accessed | tf_op | source)
XLA Modules:
  0.0 124.0 jit_solution(17388343090539813440)
XLA Ops:
  0.6 119.5 %shard_map.157 = (bf16[1024,512]{1,0:T(8,128)(2,1)}, bf16[1024,512]{1,0:T(8,128)(2,1)}, bf16[16,16,128]{2,1,0:T(8,128)(2,1)}) custom-call(s32[16]{0:T(128)} %adapter_of.1, s32[4]{0:T(128)} %target_of.1, s32[4]{0:T(128)} %length_of.1, s32[1,16]{1,0:T(1,128)} %bitcast.5, bf16[2,4,512]{2,1,0:T(4,128)(2,1)} %xd.1, bf16[512,8192]{1,0:T(8,128)(2,1)} %x_hbm.1, ...), custom_call_target="tpu_custom_call" | custom-call | flops 12000000000 | bytes 30000000 | tf_op jit(solution)/shard_map/pallas_call | solution.py:811
  120.2 3.9 %shard_map.158 = (bf16[1024,512]{1,0:T(8,128)(2,1)}, bf16[1024,512]{1,0:T(8,128)(2,1)}, bf16[2,4,4096]{2,1,0:T(4,128)(2,1)}) custom-call(bf16[1024,512]{1,0:T(8,128)(2,1)} %get-tuple-element.9.pk, bf16[1024,512]{1,0:T(8,128)(2,1)} %get-tuple-element.10.pv, bf16[16,16,128]{2,1,0:T(8,128)(2,1)} %get-tuple-element.11.att), custom_call_target="tpu_custom_call" | custom-call | tf_op jit(solution)/shard_map/pallas_call | solution.py:893

commit v4 on v3

--- a/solution.py
+++ b/solution.py
@@ -36,14 +36,16 @@
 DBLOCKS = 48
 PER = 3
 
-PROJECT_AT = (9, 11, 12, 13, 14, 15, 17, 18)
-PLACE_AT = tuple(at + 2 for at in PROJECT_AT)
-LAND_AT = tuple(at + 4 for at in PROJECT_AT)
-CACHE_AT = (10, 14, 16, 18)
-ADD_LAG = (3, 5, 7, 8)
+STEPS_AT = ((9, 0, 1), (12, 1, 3), (13, 3, 5), (17, 5, 7))
+PLACES = (13, 15, 17, 19)
+LANDS = (18, 19, 20, 21)
+FAR = 7
+PLACE_LAG = 2
+LAND_LAG = 6
+CACHE_AT = (18, 19, 20, 21)
 ACROSS_AT = (9, 11, 12, 12)
-FAR_AT = (15, 17, 18, 18)
-LAST = LAND_AT[-1]
+FAR_AT = 18
+LAST = 21
 
 MESH = pl.DeviceIdType.MESH
 F32 = jnp.float32
@@ -207,11 +209,14 @@
         load.wait()
 
     def block_of(h):
-        u = h // 2
-        return jnp.where(u == 0, HEADS + s, u - 1)
+        key = (h - 2) // 4 * 2 + lax.rem(h, 2)
+        return jnp.where(h < 2, HEADS + s, key)
+
+    def half_of(h):
+        return jnp.where(h < 2, h, lax.rem((h - 2) // 2, 2))
 
     def pass_on(h, stage, shard, first, count, ctx):
-        start = shard * SHARD + lax.rem(h, 2) * HALF + first
+        start = shard * SHARD + half_of(h) * HALF + first
         piece = w_v.at[block_of(h), pl.ds(pl.multiple_of(start, 64), count)]
         send(piece, piece, g_send.at[h], g_recv.at[h, stage], here(ctx))
 
@@ -314,6 +319,7 @@
             send(piece, piece, small_send.at[7], small_recv.at[7], here(ctx))
 
     def project_down():
+        x_copy.wait()
         for load in ups:
             load.wait()
         wait_bytes(dt_v.at[:, pl.ds(0, (N_CTX - 1) * SHARD)], small_recv.at[7])
@@ -328,71 +334,87 @@
         dn[t] = jnp.dot(down, pick, preferred_element_type=F32).astype(BF16)
         send(dn.at[t], dn.at[t], small_send.at[1], small_recv.at[1], partner)
 
-    def add_shards(n, shards, first, count):
-        parts = [
-            pl.ds(pl.multiple_of(shard * SHARD + first, HALF), count) for shard in shards
-        ]
-
-        @pl.loop(0, 2)
-        def _(m):
-            some = pl.ds(pl.multiple_of(m * 256, 256), 256)
-            hidden = jnp.concatenate([x_v[some, part] for part in parts], axis=1)
-            weight = jnp.concatenate([w_v[n, part] for part in parts], axis=0)
-            accs[n, some] += jnp.dot(hidden, weight, preferred_element_type=F32)
-
-    def add_across(group):
-        shards = GROUPS[group] + ((c,) if group == 0 else ())
-        add_shards(HEADS + s_left, shards, 0, SHARD)
-        add_shards(HEADS + s_right, shards, 0, SHARD)
-
-    def add_far(group):
-        count = len(GROUPS[group])
+    def add(blocks, hidden_parts, rounds):
+        @pl.loop(0, rounds)
+        def _(i):
+            parts = hidden_parts(i)
+            hidden = jnp.concatenate([x_v[:, part] for part in parts], axis=1)
+            weight = jnp.concatenate(
+                [jnp.concatenate([w_v[n, part] for n in blocks], axis=1) for part in parts],
+                axis=0,
+            )
+            product = jnp.dot(hidden, weight, preferred_element_type=F32)
+            for j, n in enumerate(blocks):
+                accs[n] += product[:, j * HD : (j + 1) * HD]
+
+    def whole(i):
+        return [pl.ds(pl.multiple_of(i * 2048, 2048), 2048)]
+
+    def half_rows(half):
+        def parts(i):
+            return [
+                pl.ds(pl.multiple_of((i * 8 + j) * SHARD + half * HALF, HALF), HALF)
+                for j in range(8)
+            ]
+
+        return parts
+
+    def wait_far():
         n = HEADS + s_far
-        wait_bytes(w_v.at[n, pl.ds(0, count * CUT)], f_recv.at[0, group])
-        wait_bytes(w_v.at[n, pl.ds(0, count * (SHARD - CUT))], f_recv.at[1, group])
-        add_shards(n, GROUPS[group] + ((c,) if group == 0 else ()), 0, SHARD)
+        for group in range(4):
+            count = len(GROUPS[group])
+            wait_bytes(w_v.at[n, pl.ds(0, count * CUT)], f_recv.at[0, group])
+            wait_bytes(w_v.at[n, pl.ds(0, count * (SHARD - CUT))], f_recv.at[1, group])
 
     def nth(p, sec):
-        keys = jnp.where(p == 6, 3, p // 2)
-        ahead = jnp.where(p == 2, n_sec - 1, jnp.where(p == 4, 1, jnp.where(p == 7, 2, 0)))
-        is_key = (p == 1) | (p == 3) | (p == 5) | (p == 6)
-        return jnp.where(is_key, keys, HEADS + lax.rem(sec + ahead, n_sec))
+        ahead = jnp.where(p == 0, 0, jnp.where(p == 1, n_sec - 1, jnp.where(p == 2, 1, 2)))
+        is_key = (p >= 3) & (p < 3 + HEADS)
+        return jnp.where(is_key, p - 3, HEADS + lax.rem(sec + ahead, n_sec))
 
     def project(p):
         n = nth(p, s)
 
-        @pl.when(p == 0)
-        def _():
+        if p == 0:
             wait_bytes(dn.at[0], small_recv.at[1])
 
         delta = jnp.dot(dn[n // HEADS], up_v[n], preferred_element_type=F32)
-        row[n] = (accs[n] + ADAPTER_SCALE * delta).astype(BF16)
-        send(row.at[n], raw.at[n], row_send.at[n], row_recv.at[n], right)
-
-    def exchange(n):
+        row[p] = (accs[n] + ADAPTER_SCALE * delta).astype(BF16)
+
+    def ship(first, end):
+        some = pl.ds(first, end - first)
+        send(row.at[some], raw.at[some], row_send.at[first], row_recv.at[first], right)
+
+    def exchange(first, end):
+        some = pl.ds(first, end - first)
+        ours = pl.ds(pl.multiple_of(c * PAIR, PAIR), PAIR)
+
         @pl.loop(1, N_CTX)
         def _(j):
             ctx = lax.rem(c + j, N_CTX)
             theirs = pl.ds(pl.multiple_of(ctx * PAIR, PAIR), PAIR)
-            ours = pl.ds(pl.multiple_of(c * PAIR, PAIR), PAIR)
             send(
-                sendb.at[n, theirs], pages.at[n, ours], a_send.at[n], a_recv.at[n], here(ctx)
+                sendb.at[some, theirs],
+                pages.at[some, ours],
+                a_send.at[first],
+                a_recv.at[first],
+                here(ctx),
             )
 
-        ours = pl.ds(pl.multiple_of(c * PAIR, PAIR), PAIR)
-        pages[n, ours] = sendb[n, ours]
-
-    def place(n):
-        wait_bytes(raw.at[n], row_recv.at[n])
+        for p in range(first, end):
+            pages[p, ours] = sendb[p, ours]
+
+    def place(first, end):
+        wait_bytes(raw.at[pl.ds(first, end - first)], row_recv.at[first])
 
         @pl.loop(0, 4)
         def _(i):
             some = pl.ds(pl.multiple_of(i * 256, 256), 256)
-            sendb[n, some] = jnp.dot(
-                place_m[some], raw[n], preferred_element_type=F32
-            ).astype(BF16)
-
-        exchange(n)
+            rows = jnp.concatenate([raw[p] for p in range(first, end)], axis=1)
+            placed = jnp.dot(place_m[some], rows, preferred_element_type=F32).astype(BF16)
+            for j in range(end - first):
+                sendb[first + j, some] = placed[:, j * HD : (j + 1) * HD]
+
+        exchange(first, end)
 
     def page_rows():
         first = lax.broadcasted_iota(jnp.int32, (16, 16), 0)
@@ -423,21 +445,23 @@
             flag = jnp.max(jnp.where(hit, 1.0, 0.0), axis=1, keepdims=True)
             sendb[8, some] = jnp.broadcast_to(flag, (256, HD)).astype(BF16)
 
-        exchange(8)
-
-    def landed(n):
-        wait_bytes(pages.at[n, pl.ds(0, SLOT_ROWS - PAIR)], a_recv.at[n])
-
-    def write_out(n):
+        exchange(8, 9)
+
+    def landed(first, end):
+        some = pl.ds(first, end - first)
+        wait_bytes(pages.at[some, pl.ds(0, SLOT_ROWS - PAIR)], a_recv.at[first])
+
+    def write_out(p):
+        n = nth(p, s_left)
         cols = pl.ds(pl.multiple_of(lax.rem(n, HEADS) * HD, HD), HD)
 
         @pl.when(n < HEADS)
         def _():
-            pltpu.make_async_copy(pages.at[n], pk_out.at[:, cols], out_sem.at[n]).start()
+            pltpu.make_async_copy(pages.at[p], pk_out.at[:, cols], out_sem.at[p]).start()
 
         @pl.when(n >= HEADS)
         def _():
-            pltpu.make_async_copy(pages.at[n], pv_out.at[:, cols], out_sem.at[n]).start()
+            pltpu.make_async_copy(pages.at[p], pv_out.at[:, cols], out_sem.at[p]).start()
 
     def decode_project():
         q_copy.wait()
@@ -551,12 +575,13 @@
 
     page_request = target_of[s_left] - s * RPG
 
-    def page_scores(k):
+    def page_scores(p):
+        k = nth(p, s_left)
         live = nt_dot(jnp.ones((16, HD), BF16), pages[8]) > 0.5
         query = jnp.zeros((16, HD), F32)
         for b in range(RPG):
             query = jnp.where(page_request == b, qp[k, b * 16 : b * 16 + 16].astype(F32), query)
-        scores = nt_dot(query.astype(BF16), pages[k]) * INV_ROOT
+        scores = nt_dot(query.astype(BF16), pages[p]) * INV_ROOT
         p_max = jnp.max(jnp.where(live, scores, NEG_FLOOR), axis=1, keepdims=True)
         weights = jnp.where(live, jnp.exp(scores - p_max), 0.0).astype(BF16)
         p_total = jnp.sum(weights.astype(F32), axis=1, keepdims=True)
@@ -564,8 +589,9 @@
         pgs[0, k] = jnp.broadcast_to(p_max, (16, HD))
         pgs[1, k] = jnp.broadcast_to(p_total, (16, HD))
 
-    def page_merge(k):
-        p_out = jnp.dot(pgw[k], pages[HEADS + k], preferred_element_type=F32)
+    def page_merge(p):
+        k = nth(p, s_left) - HEADS
+        p_out = jnp.dot(pgw[k], pages[p], preferred_element_type=F32)
         lane = lax.broadcasted_iota(jnp.int32, (16, HD), 1)
         for b in range(RPG):
             rows = slice(b * 16, b * 16 + 16)
@@ -591,7 +617,7 @@
     page_rows()
     accs[...] = jnp.zeros_like(accs)
 
-    @pl.loop(2, LAST)
+    @pl.loop(2, LAST + 1)
     def _(i):
         @pl.when((i >= 6) & (i < HALVES + 6))
         def _():
@@ -625,94 +651,95 @@
             def _(group=group):
                 across_again(group)
 
-        @pl.when(i == ADD_LAG[0])
-        def _():
-            x_copy.wait()
-
-        for stage, lag in enumerate(ADD_LAG):
-
-            @pl.when((i >= lag) & (i < HALVES + lag))
-            def _(stage=stage, lag=lag):
-                shards = GROUPS[stage] + ((c,) if stage == 0 else ())
-                h = i - lag
-                add_shards(block_of(h), shards, lax.rem(h, 2) * HALF, HALF)
-
-        for group, at in enumerate(ACROSS_AT):
+        @pl.when(i == 4)
+        def _():
+            decode_project()
+
+        @pl.when(i == 5)
+        def _():
+            decode_spread()
+
+        @pl.when(i == 6)
+        def _():
+            page_flags()
+
+        @pl.when(i == 7)
+        def _():
+            decode_sum()
+
+        @pl.when(i == 8)
+        def _():
+            project_down()
+
+        @pl.when(i == 9)
+        def _():
+            add((HEADS + s,), whole, 4)
+
+        @pl.when(i == 12)
+        def _():
+            add((HEADS + s_left, HEADS + s_right), whole, 4)
+
+        for at in (11, 13, 15, 17):
 
             @pl.when(i == at)
-            def _(group=group):
-                add_across(group)
-
-        for group, at in enumerate(FAR_AT):
+            def _(at=at):
+                key = (at - 11) // 4 * 2
+                add((key, key + 1), half_rows((at - 11) // 2 % 2), 2)
+
+        for at, first, end in STEPS_AT:
 
             @pl.when(i == at)
-            def _(group=group):
-                add_far(group)
-
-        @pl.when(i == 4)
-        def _():
-            decode_project()
-
-        @pl.when(i == 5)
-        def _():
-            decode_spread()
-
-        @pl.when(i == 6)
-        def _():
-            page_flags()
-
-        @pl.when(i == 7)
-        def _():
-            decode_sum()
-
-        @pl.when(i == 8)
-        def _():
-            project_down()
-
-        now, p = turn(i, PROJECT_AT)
+            def _(first=first, end=end):
+                for p in range(first, end):
+                    project(p)
+                ship(first, end)
+
+        @pl.when(i == 9)
+        def _():
+            decode_rows()
+
+        for (_, first, end), at in zip(STEPS_AT, PLACES):
+
+            @pl.when(i == at)
+            def _(first=first, end=end):
+                place(first, end)
+
+        @pl.when(i == 18)
+        def _():
+            landed(8, 9)
+
+        @pl.when(i == FAR_AT)
+        def _():
+            wait_far()
+            add((HEADS + s_far,), whole, 4)
+            project(FAR)
+            ship(FAR, FAR + 1)
+
+        now, b = turn(i, CACHE_AT)
 
         @pl.when(now)
         def _():
-            project(p)
-
-        @pl.when(i == 9)
-        def _():
-            decode_rows()
-
-        now, q = turn(i, PLACE_AT)
-
-        @pl.when(now)
-        def _():
-            place(nth(q, s_left))
-
-        now, b = turn(i, CACHE_AT)
-
-        @pl.when(now)
-        def _():
             cache_block(b)
 
-        @pl.when(i == LAND_AT[0])
-        def _():
-            landed(8)
-
-        now, r = turn(i, LAND_AT)
-
-        @pl.when(now)
-        def _():
-            n = nth(r, s_left)
-            landed(n)
-            write_out(n)
-
-            @pl.when(n < HEADS)
-            def _():
-                page_scores(n)
-
-    for r in (0, 2, 4):
-        page_merge(nth(r, s_left) - HEADS)
-    far = nth(BLOCKS - 1, s_left)
-    landed(far)
-    page_merge(far - HEADS)
-    write_out(far)
+        @pl.when(i == 20)
+        def _():
+            place(FAR, FAR + 1)
+
+        for (_, first, end), at in zip(STEPS_AT, LANDS):
+
+            @pl.when(i == at)
+            def _(first=first, end=end):
+                landed(first, end)
+                for p in range(first, end):
+                    write_out(p)
+                    if 3 <= p < 7:
+                        page_scores(p)
+
+    for early in (0, 1, 2):
+        page_merge(early)
+    landed(FAR, FAR + 1)
+    page_merge(FAR)
+    write_out(FAR)
 
     mgr[c] = mgs[c]
     wait_bytes(mgr.at[pl.ds(0, N_CTX - 1)], small_recv.at[5])
@@ -735,9 +762,11 @@
     def _(h):
         wait_bytes(w_v.at[0, pl.ds(0, 15 * HALF)], g_send.at[h])
 
-    @pl.loop(0, BLOCKS + 1)
-    def _(u):
-        wait_bytes(sendb.at[u, pl.ds(0, SLOT_ROWS - PAIR)], a_send.at[u])
+    for first, end in ((0, 1), (1, 3), (3, 5), (5, 7), (7, 8), (8, 9)):
+        some = pl.ds(first, end - first)
+        wait_bytes(sendb.at[some, pl.ds(0, SLOT_ROWS - PAIR)], a_send.at[first])
+        if end < 9:
+            wait_bytes(row.at[some], row_send.at[first])
 
     for d, count in ((0, CUT), (1, SHARD - CUT)):
         wait_bytes(w_v.at[0, pl.ds(0, 15 * SHARD)], x_send.at[d])
@@ -745,7 +774,6 @@
 
     @pl.loop(0, 2 * HEADS)
     def _(n):
-        wait_bytes(row.at[n], row_send.at[n])
         wait_bytes(pages.at[n], out_sem.at[n])
 
     wait_bytes(drow, small_send.at[0])

time: 124 us -> 121 us (0.976)
  Pallas kernels: 123 us -> 120 us
    pallas_call x1, Pallas kernels: 120 us -> 116 us  [on_device(): pl.pallas_call(layer_kernel, out_shape=(jax.ShapeDtypeStruct((SLOT_ROWS,...]
where the time goes in v4:
time: 121 us; the launch traced here: 120 us
  Pallas kernels  120 us (99%)
    pallas_call x1, Pallas kernels, on_device(): pl.pallas_call(layer_kernel, out_shape=(jax.ShapeDtypeStruct((SLOT_ROWS,...  116 us
    pallas_call x1, Pallas kernels, on_device(): pl.pallas_call(finish_kernel, out_shape=(jax.ShapeDtypeStruct((SLOT_ROWS,...  3.86 us

profile of v4, /device:TPU:0, one launch (start us, length us, event | category | flops | bytes accessed | tf_op | source)
XLA Modules:
  0.0 120.2 jit_solution(16409683355915060950)
XLA Ops:
  0.6 115.7 %shard_map.157 = (bf16[1024,512]{1,0:T(8,128)(2,1)}, bf16[1024,512]{1,0:T(8,128)(2,1)}, bf16[16,16,128]{2,1,0:T(8,128)(2,1)}) custom-call(s32[16]{0:T(128)} %adapter_of.1, s32[4]{0:T(128)} %target_of.1, s32[4]{0:T(128)} %length_of.1, s32[1,16]{1,0:T(1,128)} %bitcast.5, bf16[2,4,512]{2,1,0:T(4,128)(2,1)} %xd.1, bf16[512,8192]{1,0:T(8,128)(2,1)} %x_hbm.1, ...), custom_call_target="tpu_custom_call" | custom-call | flops 12000000000 | bytes 30000000 | tf_op jit(solution)/shard_map/pallas_call | solution.py:839
  116.4 3.9 %shard_map.158 = (bf16[1024,512]{1,0:T(8,128)(2,1)}, bf16[1024,512]{1,0:T(8,128)(2,1)}, bf16[2,4,4096]{2,1,0:T(4,128)(2,1)}) custom-call(bf16[1024,512]{1,0:T(8,128)(2,1)} %get-tuple-element.9.pk, bf16[1024,512]{1,0:T(8,128)(2,1)} %get-tuple-element.10.pv, bf16[16,16,128]{2,1,0:T(8,128)(2,1)} %get-tuple-element.11.att), custom_call_target="tpu_custom_call" | custom-call | tf_op jit(solution)/shard_map/pallas_call | solution.py:921

commit v5 on v4

--- a/solution.py
+++ b/solution.py
@@ -29,6 +29,7 @@
 HEADS = 4
 ROWS = 512
 SLOT_ROWS = 1024
+FLAG_ROWS = 256
 PAIR = 64
 RPG = 4
 CTX_DEV = 1024
@@ -105,6 +106,9 @@
     drow_r,
     sendb,
     pages,
+    flag_s,
+    flag_r,
+    live_v,
     part,
     rsr,
     ag,
@@ -442,10 +446,28 @@
             slot_row = lax.broadcasted_iota(jnp.int32, (256, ROWS), 0) + i * 256
             hit = slot_row == drow_r[0:1]
             place_m[some] = jnp.where(hit, 1.0, 0.0).astype(BF16)
-            flag = jnp.max(jnp.where(hit, 1.0, 0.0), axis=1, keepdims=True)
-            sendb[8, some] = jnp.broadcast_to(flag, (256, HD)).astype(BF16)
-
-        exchange(8, 9)
+
+        slot = lax.broadcasted_iota(jnp.int32, (FLAG_ROWS, ROWS), 0) // 8
+        taken = jnp.where(drow_r[0:1] == slot * BLK, 1.0, 0.0)
+        flag = jnp.max(taken, axis=1, keepdims=True)
+        flag_s[...] = jnp.broadcast_to(flag, (FLAG_ROWS, HD)).astype(BF16)
+        ours = pl.ds(pl.multiple_of(c * 16, 16), 16)
+
+        @pl.loop(1, N_CTX)
+        def _(j):
+            ctx = lax.rem(c + j, N_CTX)
+            theirs = pl.ds(pl.multiple_of(ctx * 16, 16), 16)
+            send(flag_s.at[theirs], flag_r.at[ours], a_send.at[8], a_recv.at[8], here(ctx))
+
+        flag_r[ours] = flag_s[ours]
+
+    def page_live():
+        wait_bytes(flag_r.at[pl.ds(0, FLAG_ROWS - 16)], a_recv.at[8])
+        flags = nt_dot(jnp.ones((16, HD), BF16), flag_r[...]).astype(BF16)
+        at = lax.broadcasted_iota(jnp.int32, (FLAG_ROWS, SLOT_ROWS), 0)
+        to = lax.broadcasted_iota(jnp.int32, (FLAG_ROWS, SLOT_ROWS), 1)
+        spread = jnp.where((lax.rem(at, 8) == 0) & (at // 8 == to // BLK), 1.0, 0.0)
+        live_v[...] = jnp.dot(flags, spread.astype(BF16), preferred_element_type=F32)
 
     def landed(first, end):
         some = pl.ds(first, end - first)
@@ -577,7 +599,7 @@
 
     def page_scores(p):
         k = nth(p, s_left)
-        live = nt_dot(jnp.ones((16, HD), BF16), pages[8]) > 0.5
+        live = live_v[...] > 0.5
         query = jnp.zeros((16, HD), F32)
         for b in range(RPG):
             query = jnp.where(page_request == b, qp[k, b * 16 : b * 16 + 16].astype(F32), query)
@@ -706,7 +728,7 @@
 
         @pl.when(i == 18)
         def _():
-            landed(8, 9)
+            page_live()
 
         @pl.when(i == FAR_AT)
         def _():
@@ -762,11 +784,12 @@
     def _(h):
         wait_bytes(w_v.at[0, pl.ds(0, 15 * HALF)], g_send.at[h])
 
-    for first, end in ((0, 1), (1, 3), (3, 5), (5, 7), (7, 8), (8, 9)):
+    for first, end in ((0, 1), (1, 3), (3, 5), (5, 7), (7, 8)):
         some = pl.ds(first, end - first)
         wait_bytes(sendb.at[some, pl.ds(0, SLOT_ROWS - PAIR)], a_send.at[first])
-        if end < 9:
-            wait_bytes(row.at[some], row_send.at[first])
+        wait_bytes(row.at[some], row_send.at[first])
+
+    wait_bytes(flag_s.at[pl.ds(0, FLAG_ROWS - 16)], a_send.at[8])
 
     for d, count in ((0, CUT), (1, SHARD - CUT)):
         wait_bytes(w_v.at[0, pl.ds(0, 15 * SHARD)], x_send.at[d])
@@ -863,8 +886,11 @@
             pltpu.VMEM((SLOT_ROWS, ROWS), BF16),
             pltpu.VMEM((8, ROWS), jnp.int32),
             pltpu.VMEM((8, ROWS), jnp.int32),
-            pltpu.VMEM((9, SLOT_ROWS, HD), BF16),
-            pltpu.VMEM((9, SLOT_ROWS, HD), BF16),
+            pltpu.VMEM((BLOCKS, SLOT_ROWS, HD), BF16),
+            pltpu.VMEM((BLOCKS, SLOT_ROWS, HD), BF16),
+            pltpu.VMEM((FLAG_ROWS, HD), BF16),
+            pltpu.VMEM((FLAG_ROWS, HD), BF16),
+            pltpu.VMEM((16, SLOT_ROWS), F32),
             pltpu.VMEM((DBLOCKS, 8, HD), F32),
             pltpu.VMEM((N_CTX, PER, 8, HD), F32),
             pltpu.VMEM((DBLOCKS, 8, HD), F32),

time: 121 us -> 121 us (level)
  no operation moved by 1% of the time
where the time goes in v5:
time: 121 us; the launch traced here: 119 us
  Pallas kernels  119 us (98%)
    pallas_call x1, Pallas kernels, on_device(): pl.pallas_call(layer_kernel, out_shape=(jax.ShapeDtypeStruct((SLOT_ROWS,...  115 us
    pallas_call x1, Pallas kernels, on_device(): pl.pallas_call(finish_kernel, out_shape=(jax.ShapeDtypeStruct((SLOT_ROWS,...  3.86 us

profile of v5, /device:TPU:0, one launch (start us, length us, event | category | flops | bytes accessed | tf_op | source)
XLA Modules:
  0.0 119.2 jit_solution(1429250596800841042)
XLA Ops:
  0.6 114.7 %shard_map.157 = (bf16[1024,512]{1,0:T(8,128)(2,1)}, bf16[1024,512]{1,0:T(8,128)(2,1)}, bf16[16,16,128]{2,1,0:T(8,128)(2,1)}) custom-call(s32[16]{0:T(128)} %adapter_of.1, s32[4]{0:T(128)} %target_of.1, s32[4]{0:T(128)} %length_of.1, s32[1,16]{1,0:T(1,128)} %bitcast.5, bf16[2,4,512]{2,1,0:T(4,128)(2,1)} %xd.1, bf16[512,8192]{1,0:T(8,128)(2,1)} %x_hbm.1, ...), custom_call_target="tpu_custom_call" | custom-call | flops 12000000000 | bytes 30000000 | tf_op jit(solution)/shard_map/pallas_call | solution.py:862
  115.3 3.9 %shard_map.158 = (bf16[1024,512]{1,0:T(8,128)(2,1)}, bf16[1024,512]{1,0:T(8,128)(2,1)}, bf16[2,4,4096]{2,1,0:T(4,128)(2,1)}) custom-call(bf16[1024,512]{1,0:T(8,128)(2,1)} %get-tuple-element.9.pk, bf16[1024,512]{1,0:T(8,128)(2,1)} %get-tuple-element.10.pv, bf16[16,16,128]{2,1,0:T(8,128)(2,1)} %get-tuple-element.11.att), custom_call_target="tpu_custom_call" | custom-call | tf_op jit(solution)/shard_map/pallas_call | solution.py:947

commit v6 on v5

--- a/solution.py
+++ b/solution.py
@@ -43,7 +43,7 @@
 FAR = 7
 PLACE_LAG = 2
 LAND_LAG = 6
-CACHE_AT = (18, 19, 20, 21)
+CACHE_AT = (15, 16, 18, 19)
 ACROSS_AT = (9, 11, 12, 12)
 FAR_AT = 18
 LAST = 21

time: 121 us -> 121 us (level)
  no operation moved by 1% of the time
where the time goes in v6:
time: 121 us; the launch traced here: 119 us
  Pallas kernels  119 us (98%)
    pallas_call x1, Pallas kernels, on_device(): pl.pallas_call(layer_kernel, out_shape=(jax.ShapeDtypeStruct((SLOT_ROWS,...  115 us
    pallas_call x1, Pallas kernels, on_device(): pl.pallas_call(finish_kernel, out_shape=(jax.ShapeDtypeStruct((SLOT_ROWS,...  3.86 us

profile of v6, /device:TPU:0, one launch (start us, length us, event | category | flops | bytes accessed | tf_op | source)
XLA Modules:
  0.0 119.3 jit_solution(2153515104771812034)
XLA Ops:
  0.6 114.8 %shard_map.157 = (bf16[1024,512]{1,0:T(8,128)(2,1)}, bf16[1024,512]{1,0:T(8,128)(2,1)}, bf16[16,16,128]{2,1,0:T(8,128)(2,1)}) custom-call(s32[16]{0:T(128)} %adapter_of.1, s32[4]{0:T(128)} %target_of.1, s32[4]{0:T(128)} %length_of.1, s32[1,16]{1,0:T(1,128)} %bitcast.5, bf16[2,4,512]{2,1,0:T(4,128)(2,1)} %xd.1, bf16[512,8192]{1,0:T(8,128)(2,1)} %x_hbm.1, ...), custom_call_target="tpu_custom_call" | custom-call | flops 12000000000 | bytes 30000000 | tf_op jit(solution)/shard_map/pallas_call | solution.py:862
  115.4 3.9 %shard_map.158 = (bf16[1024,512]{1,0:T(8,128)(2,1)}, bf16[1024,512]{1,0:T(8,128)(2,1)}, bf16[2,4,4096]{2,1,0:T(4,128)(2,1)}) custom-call(bf16[1024,512]{1,0:T(8,128)(2,1)} %get-tuple-element.9.pk, bf16[1024,512]{1,0:T(8,128)(2,1)} %get-tuple-element.10.pv, bf16[16,16,128]{2,1,0:T(8,128)(2,1)} %get-tuple-element.11.att), custom_call_target="tpu_custom_call" | custom-call | tf_op jit(solution)/shard_map/pallas_call | solution.py:947
